TPU v7x, 32 devices: a whole 2x2x4 slice. The times are simulated.
32 devices in a mesh: row: 4 (over y, x), col: 8 (over z, core).
Axes of the slice: x: 2, y: 2, z: 4, core: 2. Of those that a mesh axis runs over, the one named last changes fastest.
Arguments:
- tokens: bfloat16 [12608, 512], P('col', 'row'), may hold values from -3 to 3
- ln1_gain: float32 [512], P('row'), may hold values from 0.5 to 1.5
- ln1_bias: float32 [512], P('row'), may hold values from -1.5 to 1.5
- qkv_weight: bfloat16 [512, 1536], P('row', 'col'), may hold values from -0.25 to 0.25
- out_weight: bfloat16 [512, 512], P('row', 'col'), may hold values from -1 to 1
- ln2_gain: float32 [512], P('row'), may hold values from 0.5 to 1.5
- ln2_bias: float32 [512], P('row'), may hold values from -1.5 to 1.5
- router_weight: bfloat16 [512, 32], P('row'), may hold values from -0.1875 to 0.1875
- expert_in: bfloat16 [32, 512, 2048], P(None, 'row', 'col'), may hold values from -0.25 to 0.25
- expert_out: bfloat16 [32, 2048, 512], P(None, 'row', 'col'), may hold values from -2 to 2
- routes: int32 [12608, 2], P('col'), may hold values from 0 to 31, all different within a row; in each aligned block of 1576 rows (0 to 1575, 1576 to 3151, ...) at most 120 rows name the same one
- keep: int32 [12608, 2], P('col'), may hold values 0 or 1
- cotangent: bfloat16 [12608, 512], P('col', 'row'), may hold values from -6 to 6
Outputs:
- layer_out: bfloat16 [12608, 512], P('col', 'row')
- tokens_grad: float32 [12608, 512], P('col', 'row')
- ln1_gain_grad: float32 [512], P(('row', 'col'))
- ln1_bias_grad: float32 [512], P(('row', 'col'))
- qkv_grad: float32 [512, 1536], P('row', 'col')
- out_weight_grad: float32 [512, 512], P('row', 'col')
- ln2_gain_grad: float32 [512], P(('row', 'col'))
- ln2_bias_grad: float32 [512], P(('row', 'col'))
- router_grad: float32 [512, 32], P(('row', 'col'))
- expert_in_grad: float32 [32, 512, 2048], P(None, 'row', 'col')
- expert_out_grad: float32 [32, 2048, 512], P(None, 'row', 'col')
Inputs may be any that keep to these rules, and one draw needn't show every extreme that they name: `routes`: each row names two different experts. In each aligned block of 1576 rows no expert is named by more than 120 rows, and in some block some expert is named by exactly 120 rows.
All inputs are finite; a program needn't handle non-finite values. No bound on the sum of `keep` on one device may be relied on, other than what follows from the above.
Results may differ from a plain program's by a relative error of at most 0.019.
Values may be sent and summed in bfloat16 or wider, within the bound.
No kernel may reach another device: no remote copies, remote signals or barrier semaphores. Data moves between devices by JAX's collectives and lax.ppermute only.
A program may use at most 192 MiB of HBM per device.

v0:
```python
import math
from functools import partial

import jax
import jax.numpy as jnp
from jax import lax
from jax.experimental import pallas as pl
from jax.experimental.pallas import tpu as pltpu
from jax.sharding import PartitionSpec as P

E = 32
SEQ = 197
ROWS = 208
HD = 64
CAP = 120
EPS_NORM = 1e-06
VMEM = 60 * 2**20
TILE = 480
UNROLL = 4
F32 = jnp.float32
BF16 = jnp.bfloat16

def dot(a, b, dims):
    return lax.dot_general(a, b, (dims, ((), ())), preferred_element_type=F32)


def col_groups():
    rows, cols = lax.axis_size("row"), lax.axis_size("col")
    near = E // rows
    return cols // near, near


def exchange(pieces):
    groups, near = col_groups()
    if groups == 1:
        return lax.all_to_all(pieces, ("row", "col"), 0, 0, tiled=True)
    rows = lax.axis_size("row")
    index = [[g * near + c for c in range(near)] for g in range(groups)]
    parts = pieces.reshape((rows, near) + pieces.shape[1:])
    parts = lax.all_to_all(parts, "row", 0, 0, tiled=True)
    parts = lax.all_to_all(parts, "col", 1, 1, tiled=True, axis_index_groups=index)
    return parts.reshape(pieces.shape)


def far_groups():
    groups, near = col_groups()
    return [[g * near + c for g in range(groups)] for c in range(near)]


def collect_far(x):
    if col_groups()[0] == 1:
        return x[None]
    return lax.all_gather(x, "col", axis=0, axis_index_groups=far_groups())


def reduce_far(x):
    if col_groups()[0] == 1:
        return x[0]
    return lax.psum_scatter(x, "col", scatter_dimension=0, axis_index_groups=far_groups())


def after(x, *earlier):
    return lax.optimization_barrier((x,) + earlier)[0]


def swaps(axis, distance):
    return [(i, i ^ distance) for i in range(lax.axis_size(axis))]


def pick(pieces, at):
    return lax.dynamic_index_in_dim(pieces, at, 0, keepdims=False)


def in_order(got, here):
    pieces, step = list(got), 1
    while step < len(pieces):
        odd = (here & step) != 0
        pieces = [jnp.where(odd, pieces[k ^ step], pieces[k]) for k in range(len(pieces))]
        step *= 2
    return pieces


def row_exchange(pieces):
    here = lax.axis_index("row")
    got = [pick(pieces, here)]
    for k in range(1, lax.axis_size("row")):
        got.append(lax.ppermute(pick(pieces, here ^ k), "row", swaps("row", k)))
    return in_order(got, here)


def row_swap(pieces):
    got = [lax.ppermute(x, "row", swaps("row", k)) for k, x in enumerate(pieces) if k]
    return [pieces[0]] + got


def for_rows(x):
    here = lax.axis_index("row")
    return [pick(x, here ^ k) for k in range(x.shape[0])]


def row_spread(x):
    got = [x] + [lax.ppermute(x, "row", swaps("row", k)) for k in range(1, lax.axis_size("row"))]
    return jnp.stack(in_order(got, lax.axis_index("row")))


def far_swap(pieces):
    got = [lax.ppermute(x, "col", swaps("col", 2 * k)) for k, x in enumerate(pieces) if k]
    return [pieces[0]] + got


def core_swap(x):
    return lax.ppermute(x, "col", swaps("col", 1))


def parity_groups():
    cols = lax.axis_size("col")
    return [[2 * i + k for i in range(cols // 2)] for k in range(2)]


def far_spread(x):
    half = lax.axis_size("col") // 2
    if half > 8:
        return lax.all_gather(x, "col", axis=0, axis_index_groups=parity_groups())
    got = [x] + [lax.ppermute(x, "col", swaps("col", 2 * k)) for k in range(1, half)]
    return jnp.stack(in_order(got, lax.axis_index("col") // 2))


def far_sum(pieces):
    half = lax.axis_size("col") // 2
    if half > 8:
        got = lax.all_to_all(pieces, "col", 0, 0, tiled=True, axis_index_groups=parity_groups())
        return jnp.sum(got.astype(F32), axis=0)
    here = lax.axis_index("col") // 2
    total = pick(pieces, here).astype(F32)
    for k in range(1, half):
        sent = lax.ppermute(pick(pieces, here ^ k), "col", swaps("col", 2 * k))
        total = total + sent.astype(F32)
    return total


def gather_all(x):
    half = lax.axis_size("col") // 2
    mine = row_spread(x)
    other = lax.ppermute(mine, "col", swaps("col", 1))
    first = lax.axis_index("col") % 2 == 0
    both = jnp.stack([jnp.where(first, mine, other), jnp.where(first, other, mine)], axis=2)
    return both.reshape((both.shape[0], 2 * half) + x.shape[1:])


def reduce_all(x):
    cols, n, width = x.shape
    rows = lax.axis_size("row")
    core = lax.axis_index("col") % 2
    pairs = x.reshape(cols // 2, 2, n, width).transpose(1, 0, 2, 3).astype(BF16)
    sent = lax.ppermute(pick(pairs, 1 - core), "col", swaps("col", 1))
    mine = pick(pairs, core).astype(F32) + sent.astype(F32)
    mine = mine.astype(BF16).reshape(cols // 2, n, rows, width // rows).transpose(2, 0, 1, 3)
    mine = sum(piece.astype(F32) for piece in row_exchange(mine))
    return far_sum(mine.astype(BF16))


def pack_in(x, chunks):
    e, n, h = x.shape
    return x.reshape(e, chunks, n // chunks, h).transpose(0, 2, 1, 3).reshape(e, n // chunks, -1)


def unpack_in(x, chunks):
    e, n, h = x.shape
    x = x.reshape(e, n, chunks, h // chunks).transpose(0, 2, 1, 3)
    return x.reshape(e, n * chunks, h // chunks)


def pack_in(x, chunks):
    e, n, h = x.shape
    return x.reshape(e, chunks, n // chunks, h).transpose(0, 2, 1, 3).reshape(e, n // chunks, -1)


def unpack_in(x, chunks):
    e, n, h = x.shape
    x = x.reshape(e, n, chunks, h // chunks).transpose(0, 2, 1, 3)
    return x.reshape(e, n * chunks, h // chunks)


def all_experts(got, rows, near, chunks):
    groups = col_groups()[0]
    if groups == 1:
        return got
    m = got.shape[1] // 2
    k = got.shape[2]
    w_in = unpack_in(got[:, :m], chunks)
    _, n, h = w_in.shape
    w_in = collect_far(w_in.reshape(rows, near, n, h)).transpose(1, 3, 0, 2, 4)
    w_in = w_in.reshape(rows, n, near, groups * h).transpose(0, 2, 1, 3).reshape(E, n, groups * h)
    w_out_t = collect_far(got[:, m:].reshape(rows, near, m, k)).transpose(1, 0, 2, 3, 4)
    w_out_t = w_out_t.reshape(E, groups * m, k)
    return jnp.concatenate([pack_in(w_in, near // rows), w_out_t], axis=1)


def own_experts(sent, rows, near, chunks):
    groups = col_groups()[0]
    if groups == 1:
        return sent
    m = sent.shape[1] // 2
    k = sent.shape[2]
    w_in = unpack_in(sent[:, :m], near // rows)
    _, n, h = w_in.shape
    w_in = w_in.reshape(rows, near, n, h).transpose(0, 2, 1, 3)
    w_in = w_in.reshape(rows, n, groups, near, h // groups).transpose(2, 0, 3, 1, 4)
    w_in = reduce_far(w_in).reshape(E, n, h // groups)
    w_out_t = sent[:, m:].reshape(rows, groups, near, m // groups, k).transpose(1, 0, 2, 3, 4)
    w_out_t = reduce_far(w_out_t).reshape(E, m // groups, k)
    return jnp.concatenate([pack_in(w_in, chunks), w_out_t], axis=1)


def pad_images(x):
    t, w = x.shape
    return jnp.pad(x.reshape(t // SEQ, SEQ, w), ((0, 0), (0, ROWS - SEQ), (0, 0))).reshape(-1, w)


def cut_images(x):
    t, w = x.shape
    return x.reshape(t // ROWS, ROWS, w)[:, :SEQ].reshape(-1, w)


def call(kernel, name, out_shape, n_in, scalars=0, scratch=(), flops=0, moved=0, **kw):
    smem = pl.BlockSpec(memory_space=pltpu.SMEM)
    vmem = pl.BlockSpec(memory_space=pltpu.VMEM)
    return pl.pallas_call(
        kernel,
        name=name,
        out_shape=out_shape,
        in_specs=[smem] * scalars + [vmem] * n_in,
        out_specs=jax.tree.map(lambda _: vmem, out_shape),
        scratch_shapes=list(scratch),
        compiler_params=pltpu.CompilerParams(vmem_limit_bytes=VMEM),
        cost_estimate=pl.CostEstimate(flops=flops, bytes_accessed=moved, transcendentals=0),
        **kw,
    )


def shape(dims, dtype):
    return jax.ShapeDtypeStruct(tuple(dims), dtype)


def block(i, n):
    if isinstance(i, int):
        return slice(i * n, (i + 1) * n)
    return pl.ds(pl.multiple_of(i * n, n), n)


def pack_kernel(chunks, in_ref, out_ref, sent_ref):
    n = in_ref.shape[1] // chunks
    h = in_ref.shape[2]
    for c in range(chunks):
        sent_ref[:, :n, c * h : (c + 1) * h] = in_ref[:, c * n : (c + 1) * n, :]
    sent_ref[:, n:, :] = out_ref[...]


def unpack_kernel(chunks, got_ref, in_ref, out_ref):
    n = in_ref.shape[1] // chunks
    h = in_ref.shape[2]
    for c in range(chunks):
        in_ref[:, c * n : (c + 1) * n, :] = got_ref[:, :n, c * h : (c + 1) * h].astype(F32)
    out_ref[...] = got_ref[:, n:, :].astype(F32)


def pack_weights(w_in, w_out_t):
    e, n, h = w_in.shape
    _, m, k = w_out_t.shape
    step = 16
    spec = lambda a, b: pl.BlockSpec((step, a, b), lambda i: (i, 0, 0))
    return pl.pallas_call(
        partial(pack_kernel, n // m),
        name="pack_weights",
        grid=(e // step,),
        out_shape=shape((e, 2 * m, k), BF16),
        in_specs=[spec(n, h), spec(m, k)],
        out_specs=spec(2 * m, k),
        compiler_params=pltpu.CompilerParams(vmem_limit_bytes=VMEM),
        cost_estimate=pl.CostEstimate(flops=0, bytes_accessed=8 * e * m * k, transcendentals=0),
    )(w_in, w_out_t)


def unpack_grads(got, n, h):
    e, m2, k = got.shape
    m = m2 // 2
    step = 16
    spec = lambda a, b: pl.BlockSpec((step, a, b), lambda i: (i, 0, 0))
    return pl.pallas_call(
        partial(unpack_kernel, n // m),
        name="unpack_grads",
        grid=(e // step,),
        out_shape=(shape((e, n, h), F32), shape((e, m, k), F32)),
        in_specs=[spec(m2, k)],
        out_specs=(spec(n, h), spec(m, k)),
        compiler_params=pltpu.CompilerParams(vmem_limit_bytes=VMEM),
        cost_estimate=pl.CostEstimate(flops=0, bytes_accessed=12 * e * m * k, transcendentals=0),
    )(got)


def slots_kernel(routes_ref, keep_ref, slots_ref):
    tokens = routes_ref.shape[1]
    experts = lax.broadcasted_iota(jnp.int32, (E, tokens), 0)
    named = [experts == routes_ref[j : j + 1, :] for j in range(2)]
    both = jnp.where(named[0] | named[1], 1.0, 0.0).astype(BF16)
    width = 128
    upper = lax.broadcasted_iota(jnp.int32, (width, width), 0) < lax.broadcasted_iota(
        jnp.int32, (width, width), 1
    )
    upper = jnp.where(upper, 1.0, 0.0).astype(BF16)
    before = jnp.zeros((E, 1), F32)
    counts = []
    for i in range(tokens // width):
        part = both[:, i * width : (i + 1) * width]
        counts.append(dot(part, upper, ((1,), (0,))) + before)
        before = before + jnp.sum(part.astype(F32), axis=1, keepdims=True)
    place = jnp.concatenate(counts, axis=1) + (experts * CAP).astype(F32)
    for j in range(2):
        slot = jnp.sum(jnp.where(named[j], place, 0.0), axis=0, keepdims=True).astype(jnp.int32)
        slots_ref[j : j + 1, :] = jnp.where(keep_ref[j : j + 1, :] != 0, slot, -1)


def slot_table(routes, keep):
    return call(slots_kernel, "slots", shape(routes.shape, jnp.int32), 2)(routes, keep)


def dispatch_kernel(n, where_ref, slots_ref, *refs):
    pieces, (sent_ref, values) = refs[:n], refs[n:]
    here = where_ref[0]
    part = pieces[0].shape[0]
    for k in range(n):
        values[block(here ^ k, part), :] = pieces[k][...]
    tokens = values.shape[0]
    step = 4

    def experts(i, carry):
        hits = []
        for j in range(step):
            first = (i * step + j) * CAP
            place = [slots_ref[p : p + 1, :] - first for p in range(2)]
            mine = [(p >= 0) & (p < CAP) for p in place]
            at = jnp.where(mine[0], place[0], jnp.where(mine[1], place[1], -1))
            rows = lax.broadcasted_iota(jnp.int32, (CAP, tokens), 0)
            hits.append(jnp.where(rows == at, 1.0, 0.0))
        hits = jnp.concatenate(hits, axis=0).astype(BF16)
        out = dot(hits, values[...], ((1,), (0,))).astype(BF16)
        sent_ref[block(i, step * CAP), :] = out
        return carry

    lax.fori_loop(0, E // step, experts, 0)


def dispatch(here, slots, pieces):
    n = len(pieces)
    part, w = pieces[0].shape
    return call(
        partial(dispatch_kernel, n),
        "dispatch",
        shape((E * CAP, w), BF16),
        1 + n,
        scalars=1,
        scratch=[pltpu.VMEM((n * part, w), BF16)],
        flops=2 * E * CAP * n * part * w,
        moved=2 * (E * CAP + n * part) * w,
    )(here, slots, *pieces)


def combine_rows(columns, got_ref):
    places = lax.broadcasted_iota(jnp.int32, (columns.shape[0], E * CAP), 1)
    hits = (places == columns[:, 0:1]) | (places == columns[:, 1:2])
    hits = jnp.where(hits, 1.0, 0.0).astype(BF16)
    return dot(hits, got_ref[...], ((1,), (0,)))


def combine_kernel(n, where_ref, columns_ref, got_ref, *outs):
    here = where_ref[0]
    part = outs[0].shape[0]
    tile = part // 2
    for k in range(n):
        base = (here ^ k) * part
        for half in range(2):
            rows = pl.ds(pl.multiple_of(base + half * tile, tile), tile)
            out = combine_rows(columns_ref[rows, :], got_ref)
            outs[k][half * tile : (half + 1) * tile, :] = out.astype(BF16)


def combine(here, columns, got, n):
    w = got.shape[1]
    part = columns.shape[0] // n
    return call(
        partial(combine_kernel, n),
        "combine",
        tuple(shape((part, w), BF16) for _ in range(n)),
        2,
        scalars=1,
        flops=2 * E * CAP * n * part * w,
        moved=2 * (E * CAP + n * part) * w,
    )(here, columns, got)


def finish_kernel(n, where_ref, columns_ref, got_ref, tokens_ref, *refs):
    pieces, (out_ref,) = refs[:n], refs[n:]
    here = where_ref[0]
    part = pieces[0].shape[1]
    tile = part // 2
    for k in range(n):
        base = (here ^ k) * part
        for half in range(2):
            rows = pl.ds(pl.multiple_of(base + half * tile, tile), tile)
            out = combine_rows(columns_ref[rows, :], got_ref)
            out = out + pieces[k][0, half * tile : (half + 1) * tile, :].astype(F32)
            out = out + tokens_ref[rows, :].astype(F32)
            out_ref[rows, :] = out.astype(BF16)


def finish(here, columns, got, tokens, pieces):
    n = len(pieces)
    t, w = tokens.shape
    return call(
        partial(finish_kernel, n),
        "finish",
        shape((t, w), BF16),
        3 + n,
        scalars=1,
        flops=2 * E * CAP * t * w,
        moved=2 * (E * CAP + 3 * t) * w,
    )(here, columns, got, tokens, *pieces)


def means(x):
    return jnp.mean(x, axis=1, keepdims=True)


def normalize(values):
    centred = values - means(values)
    inverse = lax.rsqrt(means(centred * centred) + EPS_NORM)
    return centred * inverse, inverse


def norm_backward(grad_normed, normalized, inverse, gain):
    scaled = grad_normed * gain
    return inverse * (scaled - means(scaled) - normalized * means(scaled * normalized))


def head_scores(q_pair, k_pair, low, head):
    keys = k_pair.shape[0]
    q_head = jnp.where(low if head % 2 == 0 else ~low, q_pair, jnp.zeros_like(q_pair))
    scores = dot(q_head, k_pair, ((1,), (1,))) * HD ** (-0.5)
    real = lax.broadcasted_iota(jnp.int32, (1, keys), 1) < SEQ
    return jnp.where(real, scores, -1e30)


def forward_kernel(n, where_ref, *refs):
    pieces, others = refs[:n], refs[n : 2 * n]
    qkv_ref, mix_ref, norms_ref = refs[2 * n : 2 * n + 3]
    sends, laters = refs[2 * n + 3 : 3 * n + 3], refs[3 * n + 3 : 4 * n + 3]
    project_ref, attended_ref, residual_ref, totals_ref, x_s, n2_s, ao_s = refs[4 * n + 3 :]
    here = where_ref[0]
    w = pieces[0].shape[1]
    for k in range(n):
        x_s[:, block(here ^ k, w)] = pieces[k][...].astype(F32)
    width = n * w
    pairs = width // (2 * HD)
    low = lax.broadcasted_iota(jnp.int32, (1, 2 * HD), 1) < HD
    lanes = lax.broadcasted_iota(jnp.int32, (1, 128), 1)

    def image(i, carry):
        rows = block(i, ROWS)
        normed = normalize(x_s[rows, :])[0] * norms_ref[0:1, :] + norms_ref[1:2, :]
        project_ref[rows, :] = dot(normed.astype(BF16), qkv_ref[...], ((1,), (1,))).astype(BF16)

        def head_pair(pair, totals):
            q_pair, k_pair, v_pair = (
                project_ref[rows, block(j * pairs + pair, 2 * HD)] for j in range(3)
            )
            heads = []
            for head in range(2):
                scores = head_scores(q_pair, k_pair, low, head)
                top = jnp.max(scores, axis=1, keepdims=True)
                powers = jnp.exp(scores - top)
                total = jnp.sum(powers, axis=1, keepdims=True)
                probs = (powers / total).astype(BF16)
                heads.append(dot(probs, v_pair, ((1,), (0,))))
                totals = jnp.where(lanes == 2 * pair + head, top + jnp.log(total), totals)
            mixed = jnp.where(low, heads[0], heads[1])
            attended_ref[rows, block(pair, 2 * HD)] = mixed.astype(BF16)
            return totals

        totals = jnp.zeros((ROWS, 128), F32)
        for pair in range(pairs):
            totals = head_pair(pair, totals)
        totals_ref[rows, :] = totals
        attn_out = dot(attended_ref[rows, :], mix_ref[...], ((1,), (1,)))
        residual = x_s[rows, :] + attn_out
        residual_ref[rows, :] = residual
        normed = normalize(residual)[0] * norms_ref[2:3, :] + norms_ref[3:4, :]
        n2_s[rows, :] = normed.astype(BF16)
        ao_s[rows, :] = attn_out.astype(BF16)
        return carry

    lax.fori_loop(0, x_s.shape[0] // ROWS, image, 0)
    for k in range(n):
        sends[k][...] = n2_s[:, block(here ^ k, w)]
        laters[k][0] = ao_s[:, block(here ^ k, w)]
        laters[k][1] = others[k][...]


def attention_forward(where, pieces, others, qkv_t, mix_t, norms):
    n = len(pieces)
    t, w = pieces[0].shape
    width = n * w
    out = call(
        partial(forward_kernel, n),
        "attention_forward",
        tuple(shape((t, w), BF16) for _ in range(n))
        + tuple(shape((2, t, w), BF16) for _ in range(n))
        + (
            shape((t, 3 * width), BF16),
            shape((t, width), BF16),
            shape((t, width), F32),
            shape((t, 128), F32),
        ),
        2 * n + 3,
        scalars=1,
        scratch=[
            pltpu.VMEM((t, width), F32),
            pltpu.VMEM((t, width), BF16),
            pltpu.VMEM((t, width), BF16),
        ],
        flops=12 * t * width * width,
        moved=2**22,
    )(where, *pieces, *others, qkv_t, mix_t, norms)
    return out[:n], out[n : 2 * n], out[2 * n :]


def backward_kernel(n, far, parts, where_ref, *refs):
    grads, pieces, others = refs[:n], refs[n : 2 * n], refs[2 * n : 3 * n]
    (
        qkv_ref, mix_ref, norms_ref, project_ref, attended_ref, residual_ref, totals_ref, router_ref,
    ) = refs[3 * n : 3 * n + 8]
    sends = refs[3 * n + 8 : 4 * n + 8]
    refs = refs[4 * n + 8 :]
    outs, (x_s, c_s, g_s, n1_s, ga_s, gp_s, tg_s, sums_s) = refs[:-8], refs[-8:]
    here = where_ref[0]
    w = pieces[0].shape[1]
    for k in range(n):
        x_s[:, block(here ^ k, w)] = pieces[k][...].astype(F32)
        c_s[:, block(here ^ k, w)] = others[k][1].astype(F32)
        g_s[:, block(here ^ k, w)] = grads[k][...].astype(F32)
    width = n * w
    pairs = width // (2 * HD)
    low = lax.broadcasted_iota(jnp.int32, (1, 2 * HD), 1) < HD
    lanes = lax.broadcasted_iota(jnp.int32, (1, 128), 1)
    scale = HD ** (-0.5)
    sums_s[...] = jnp.zeros_like(sums_s)

    def image(i, carry):
        rows = block(i, ROWS)
        normal2, inverse2 = normalize(residual_ref[rows, :])
        grad_norm2 = g_s[rows, :]
        sums_s[2:3, :] += jnp.sum(grad_norm2 * normal2, axis=0, keepdims=True)
        sums_s[3:4, :] += jnp.sum(grad_norm2, axis=0, keepdims=True)
        grad_resid = c_s[rows, :] + norm_backward(grad_norm2, normal2, inverse2, norms_ref[2:3, :])
        c_s[rows, :] = grad_resid
        grad_attn = grad_resid.astype(BF16)
        ga_s[rows, :] = grad_attn
        tg_s[rows, :] = dot(grad_attn, mix_ref[...], ((1,), (0,))).astype(BF16)

        def head_pair(pair, carry):
            q_pair, k_pair, v_pair = (
                project_ref[rows, block(j * pairs + pair, 2 * HD)] for j in range(3)
            )
            g_pair = tg_s[rows, block(pair, 2 * HD)]
            totals = totals_ref[rows, :]
            got = []
            for head in range(2):
                scores = head_scores(q_pair, k_pair, low, head)
                total = jnp.sum(
                    jnp.where(lanes == 2 * pair + head, totals, 0.0), axis=1, keepdims=True
                )
                probs = jnp.exp(scores - total)
                g_head = jnp.where(low if head == 0 else ~low, g_pair, jnp.zeros_like(g_pair))
                grad_probs = dot(g_head, v_pair, ((1,), (1,)))
                row_dot = jnp.sum(probs * grad_probs, axis=1, keepdims=True)
                grad_scores = (probs * (grad_probs - row_dot)).astype(BF16)
                got.append(
                    (
                        dot(grad_scores, k_pair, ((1,), (0,))) * scale,
                        dot(grad_scores, q_pair, ((0,), (0,))) * scale,
                        dot(probs.astype(BF16), g_pair, ((0,), (0,))),
                    )
                )
            for j in range(3):
                out = jnp.where(low, got[0][j], got[1][j])
                gp_s[rows, block(j * pairs + pair, 2 * HD)] = out.astype(BF16)
            return carry

        lax.fori_loop(0, pairs, head_pair, 0, unroll=UNROLL)
        normal1, inverse1 = normalize(x_s[rows, :])
        n1_s[rows, :] = (normal1 * norms_ref[0:1, :] + norms_ref[1:2, :]).astype(BF16)
        grad_norm1 = dot(gp_s[rows, :], qkv_ref[...], ((1,), (0,)))
        sums_s[0:1, :] += jnp.sum(grad_norm1 * normal1, axis=0, keepdims=True)
        sums_s[1:2, :] += jnp.sum(grad_norm1, axis=0, keepdims=True)
        tokens_grad = c_s[rows, :] + norm_backward(
            grad_norm1, normal1, inverse1, norms_ref[0:1, :]
        )
        tg_s[rows, :] = tokens_grad.astype(BF16)
        return carry

    lax.fori_loop(0, x_s.shape[0] // ROWS, image, 0)
    for k in range(n):
        sends[k][...] = tg_s[:, block(here ^ k, w)]
    qkv_grad = dot(gp_s[...], n1_s[...], ((0,), (0,)))
    mix_grad = dot(ga_s[...], attended_ref[...], ((0,), (0,)))
    if parts is None:
        outs[0][...] = qkv_grad
        outs[1][...] = mix_grad
        outs[2][:E, :] = router_ref[...]
        outs[2][E : E + 8, :] = sums_s[...]
        return
    outs, (qkv_s, mix_s, small_s) = outs[:2], outs[2:]
    qkv_s[...] = qkv_grad.astype(BF16)
    mix_s[...] = mix_grad.astype(BF16)
    small_s[...] = jnp.concatenate(
        [router_ref[...], sums_s[...], jnp.zeros((8, width), F32)], axis=0
    ).astype(BF16)
    first, second = parts

    def piece(at, carry):
        k, z = at // far, at % far
        part = block(here ^ k, w)
        for p in range(2):
            c = 2 * (where_ref[1] ^ z) + (where_ref[2] ^ p)
            outs[p][k, z, :first, :] = qkv_s[block(c, first), part]
            outs[p][k, z, first : first + second, :] = mix_s[block(c, second), part]
            outs[p][k, z, first + second :, :] = small_s[:, part]
        return carry

    lax.fori_loop(0, n * far, piece, 0)


def attention_backward(
    where, grads, pieces, others, qkv_t, mix_t, norms, saved, router_part, far, parts
):
    n = len(pieces)
    t, w = pieces[0].shape
    width = n * w
    scratch = [pltpu.VMEM((t, width), F32)] * 3 + [pltpu.VMEM((t, width), BF16)] * 2
    scratch += [pltpu.VMEM((t, 3 * width), BF16), pltpu.VMEM((t, width), BF16)]
    scratch += [pltpu.VMEM((8, width), F32)]
    if parts is None:
        outs = (
            shape((3 * width, width), F32),
            shape((width, width), F32),
            shape((E + 8, width), F32),
        )
    else:
        outs = (shape((n, far, sum(parts) + E + 16, w), BF16),) * 2
        scratch = [
            pltpu.VMEM((3 * width, width), BF16),
            pltpu.VMEM((width, width), BF16),
            pltpu.VMEM((E + 16, width), BF16),
        ] + scratch
    out = call(
        partial(backward_kernel, n, far, parts),
        "attention_backward",
        tuple(shape((t, w), BF16) for _ in range(n)) + outs,
        3 * n + 8,
        scalars=1,
        scratch=scratch,
        flops=30 * t * width * width,
        moved=2**23,
    )(where, *grads, *pieces, *others, qkv_t, mix_t, norms, *saved, router_part)
    return out[:n], out[n:]


def split_three(x):
    parts = []
    for _ in range(3):
        part = lax.reduce_precision(x, 8, 7)
        parts.append(part.astype(BF16))
        x = x - part
    return parts


def gather_kernel(n, far, parts, where_ref, *refs):
    qkv_ref, mix_ref, router_ref, norms_ref = refs[2 * n :]
    first, second = parts
    depth = first + second
    w = refs[0].shape[1]
    for k in range(n):
        part = block(where_ref[0] ^ k, w)
        for p in range(2):
            piece = refs[p * n + k]
            for z in range(far):
                c = 2 * (where_ref[1] ^ z) + (where_ref[2] ^ p)
                qkv_ref[block(c, first), part] = piece[z * depth : z * depth + first, :]
                mix_ref[block(c, second), part] = piece[z * depth + first : (z + 1) * depth, :]
        router_ref[:, part] = refs[k][far * depth : far * depth + E, :]
        extra = refs[k][far * depth + E :, :].astype(F32)
        norms_ref[:, part] = extra[0:4] + extra[4:8] + extra[8:12]


def gather_weights(where, pieces, far, parts):
    n = len(pieces) // 2
    _, w = pieces[0].shape
    return call(
        partial(gather_kernel, n, far, parts),
        "gather_weights",
        tuple(shape((2 * far * part, n * w), BF16) for part in parts)
        + (shape((E, n * w), BF16), shape((4, n * w), F32)),
        2 * n,
        scalars=1,
        moved=2**22,
    )(where, *pieces)


def add_core_kernel(own_ref, got_ref, *outs):
    for k, out in enumerate(outs):
        out[...] = (own_ref[k].astype(F32) + got_ref[k].astype(F32)).astype(BF16)


def add_core(own, got):
    return call(
        add_core_kernel,
        "add_core",
        tuple(shape(own.shape[1:], BF16) for _ in range(own.shape[0])),
        2,
        moved=6 * own.size,
    )(own, got)


def add_rows_kernel(n, *refs):
    pieces, outs = refs[:n], refs[n:]
    for z, out in enumerate(outs):
        out[...] = sum(piece[z].astype(F32) for piece in pieces).astype(BF16)


def add_rows(pieces):
    far, depth, w = pieces[0].shape
    return call(
        partial(add_rows_kernel, len(pieces)),
        "add_rows",
        tuple(shape((depth, w), BF16) for _ in range(far)),
        len(pieces),
        moved=10 * far * depth * w,
    )(*pieces)


def add_far_kernel(n, parts, *refs):
    pieces, (qkv_ref, mix_ref, small_ref) = refs[:n], refs[n:]
    total = sum(piece[...].astype(F32) for piece in pieces)
    first, second = parts
    qkv_ref[...] = total[:first]
    mix_ref[...] = total[first : first + second]
    small_ref[...] = total[first + second : first + second + E + 8]


def add_far(pieces, parts):
    w = pieces[0].shape[1]
    return call(
        partial(add_far_kernel, len(pieces), parts),
        "add_far",
        tuple(shape((part, w), F32) for part in (*parts, E + 8)),
        len(pieces),
        moved=12 * pieces[0].size,
    )(*pieces)


def hidden_block(w_ref, i, rows, near):
    m = w_ref.shape[1] // 2
    k = w_ref.shape[2]
    per = near // rows
    chunks = per
    h = k // chunks
    columns = []
    for c in range(per):
        columns.append(
            jnp.concatenate(
                [
                    w_ref[r * near + i * per + c, :m, j * h : (j + 1) * h]
                    for r in range(rows)
                    for j in range(chunks)
                ],
                axis=0,
            )
        )
    w_in = jnp.concatenate(columns, axis=1)
    w_out_t = jnp.concatenate([w_ref[i * near + c, m:, :] for c in range(near)], axis=0)
    return w_in, w_out_t


def assemble(got_ref, rows_s, rows, near):
    w = got_ref.shape[2]
    for c in range(near):
        for r in range(rows):
            rows_s[c * CAP : (c + 1) * CAP, r * w : (r + 1) * w] = got_ref[r * near + c].astype(F32)


def disperse(values_s, sent_ref, rows, near):
    w = sent_ref.shape[2]
    for c in range(near):
        for r in range(rows):
            piece = values_s[c * CAP : (c + 1) * CAP, r * w : (r + 1) * w]
            sent_ref[r * near + c] = piece.astype(BF16)


ERF = (0.254829592, -0.284496736, 1.421413741, -1.453152027, 1.061405429)


def gelu_pair(x):
    size = jnp.abs(x)
    t = 1.0 / (1.0 + (0.3275911 * 0.5**0.5) * size)
    bell = jnp.exp(-0.5 * x * x)
    tail = ERF[4]
    for coefficient in ERF[3::-1]:
        tail = tail * t + coefficient
    tail = (0.5 * tail) * (t * bell)
    below = jnp.where(x < 0, tail, 1.0 - tail)
    return x * below, below + x * bell * (0.5 / math.pi) ** 0.5


def expert_forward_kernel(
    rows, near, e_ref, got_ref, w_ref, router_ref,
    sent_ref, x_ref, act_ref, slope_ref, res_ref, gates_ref, f_s, in_s, out_s,
):
    assemble(got_ref, f_s, rows, near)
    x_ref[...] = f_s[...].astype(BF16)
    logits = dot(x_ref[...], router_ref[...], ((1,), (1,)))
    powers = jnp.exp(logits - jnp.max(logits, axis=1, keepdims=True))
    gates = powers / jnp.sum(powers, axis=1, keepdims=True)
    gates_ref[...] = gates
    res_ref[...] = jnp.zeros_like(res_ref)

    def step(i, carry):
        in_s[...], out_s[...] = hidden_block(w_ref, i, rows, near)

        def tile(j, carry):
            at = block(j, TILE)
            pre = dot(x_ref[at, :], in_s[...], ((1,), (0,)))
            act, slope = gelu_pair(pre)
            act = act.astype(BF16)
            act_ref[i, at, :] = act
            slope_ref[i, at, :] = slope.astype(BF16)
            res_ref[at, :] += dot(act, out_s[...], ((1,), (1,)))
            return carry

        return lax.fori_loop(0, x_ref.shape[0] // TILE, tile, carry)

    lax.fori_loop(0, rows, step, 0)
    own = lax.broadcasted_iota(jnp.int32, (1, E), 1) == e_ref[0]
    chosen = jnp.sum(jnp.where(own, gates, 0.0), axis=1, keepdims=True)
    f_s[...] = chosen * res_ref[...]
    disperse(f_s, sent_ref, rows, near)


def expert_forward(expert, got, w_got, router_t, rows, near):
    e, _, w = got.shape
    n, width, part = near * CAP, rows * w, w_got.shape[2]
    return call(
        partial(expert_forward_kernel, rows, near),
        "expert_forward",
        (
            shape(got.shape, BF16),
            shape((n, width), BF16),
            shape((rows, n, part), BF16),
            shape((rows, n, part), BF16),
            shape((n, width), F32),
            shape((n, E), F32),
        ),
        3,
        scalars=1,
        scratch=[pltpu.VMEM((n, width), F32)] + [pltpu.VMEM((width, part), BF16)] * 2,
        flops=16 * n * width * rows * part // 4,
        moved=2**24,
    )(expert, got, w_got, router_t)


def expert_backward_kernel(
    rows, near, e_ref, got_ref, w_ref, router_ref, x_ref, slope_ref, res_ref, gates_ref,
    sent_ref, pre_ref, grad_res_ref, router_grad_ref, f_s,
):
    assemble(got_ref, f_s, rows, near)
    cot = f_s[...]
    gates = gates_ref[...]
    own = jnp.where(lax.broadcasted_iota(jnp.int32, (1, E), 1) == e_ref[0], 1.0, 0.0)
    chosen = jnp.sum(gates * own, axis=1, keepdims=True)
    grad_chosen = jnp.sum(cot * res_ref[...], axis=1, keepdims=True)
    grad_logits = (grad_chosen * chosen * (own - gates)).astype(BF16)
    grad_res_ref[...] = (chosen * cot).astype(BF16)
    router_grad_ref[...] = dot(grad_logits, x_ref[...], ((0,), (0,)))
    f_s[...] = dot(grad_logits, router_ref[...], ((1,), (0,)))

    def step(i, carry):
        w_in, w_out_t = hidden_block(w_ref, i, rows, near)
        grad_act = dot(grad_res_ref[...], w_out_t, ((1,), (0,)))
        grad_pre = (grad_act * slope_ref[i].astype(F32)).astype(BF16)
        pre_ref[i] = grad_pre
        f_s[...] += dot(grad_pre, w_in, ((1,), (1,)))
        return carry

    lax.fori_loop(0, rows, step, 0)
    disperse(f_s, sent_ref, rows, near)


def expert_backward(expert, got, w_got, router_t, x_rows, slope, res, gates, rows, near):
    e, _, w = got.shape
    n, width, part = near * CAP, rows * w, w_got.shape[2]
    return call(
        partial(expert_backward_kernel, rows, near),
        "expert_backward",
        (
            shape(got.shape, BF16),
            shape((rows, n, part), BF16),
            shape((n, width), BF16),
            shape((E, width), F32),
        ),
        7,
        scalars=1,
        scratch=[pltpu.VMEM((n, width), F32)],
        flops=16 * n * width * rows * part // 4,
        moved=2**24,
    )(expert, got, w_got, router_t, x_rows, slope, res, gates)


def expert_grads_kernel(rows, near, x_ref, pre_ref, grad_res_ref, act_ref, sent_ref):
    m = sent_ref.shape[1] // 2
    k = sent_ref.shape[2]
    per = near // rows
    h = k // per

    def step(i, carry):
        in_grad = dot(x_ref[...], pre_ref[i], ((0,), (0,))).astype(BF16)
        for r in range(rows):
            for c in range(per):
                for j in range(per):
                    first = (r * per + j) * m
                    sent_ref[r * near + i * per + c, :m, j * h : (j + 1) * h] = in_grad[
                        first : first + m, c * h : (c + 1) * h
                    ]
        out_grad_t = dot(grad_res_ref[...], act_ref[i], ((0,), (0,))).astype(BF16)
        for c in range(near):
            sent_ref[i * near + c, m:, :] = out_grad_t[c * m : (c + 1) * m, :]
        return carry

    lax.fori_loop(0, rows, step, 0)


def expert_grads(x_rows, grad_pre, grad_res, act, like, rows, near):
    n, width = x_rows.shape
    return call(
        partial(expert_grads_kernel, rows, near),
        "expert_grads",
        shape(like.shape, BF16),
        4,
        flops=4 * n * width * rows * like.shape[2],
        moved=2**24,
    )(x_rows, grad_pre, grad_res, act)


def local(
    tokens,
    ln1_gain,
    ln1_bias,
    qkv_weight,
    out_weight,
    ln2_gain,
    ln2_bias,
    router_weight,
    expert_in,
    expert_out,
    routes,
    keep,
    cotangent,
):
    rows, cols = lax.axis_size("row"), lax.axis_size("col")
    groups, near = col_groups()
    width_part = tokens.shape[1]
    width = width_part * rows
    hid_part = expert_in.shape[2]
    out_part = expert_out.shape[2]
    qkv_part, mix_part = qkv_weight.shape[1], out_weight.shape[1]
    chunks = width_part // out_part
    half = cols // 2
    parts = (qkv_part, mix_part)
    tiled = half <= 8 and all(part % 16 == 0 for part in (out_part, *parts))
    row, col = lax.axis_index("row"), lax.axis_index("col")
    here = jnp.stack([row, col // 2, col % 2]).astype(jnp.int32)
    nowhere = jnp.zeros((1,), jnp.int32)
    expert = (row * near + col % near).astype(jnp.int32)[None]

    near_parts = jnp.concatenate([qkv_weight.T, out_weight.T], axis=0)
    norms = jnp.stack([ln1_gain, ln1_bias, ln2_gain, ln2_bias])
    if tiled:
        shared = [router_weight.T, *split_three(norms), jnp.zeros_like(norms, BF16)]
        far = jnp.concatenate(far_swap([near_parts] * half) + shared)
    else:
        far = far_spread(near_parts)
    tok = pad_images(after(tokens, near_parts))
    cot = pad_images(after(cotangent, near_parts))
    pieces = row_swap(for_rows(tok.reshape(rows, -1, width_part)))
    cot_pieces = for_rows(cot.reshape(rows, -1, width_part))
    out_t = expert_out.transpose(0, 2, 1)
    if tiled:
        w_sent = pack_weights(expert_in, out_t)
    else:
        w_sent = jnp.concatenate([pack_in(expert_in, chunks), out_t], axis=1)
    w_got = exchange(after(w_sent, far))
    w_got = all_experts(w_got, rows, near, chunks)
    if tiled:
        mine = row_swap([far] * rows)
        qkv_t, mix_t, router_t, norms = gather_weights(
            here, mine + [core_swap(x) for x in mine], half, parts
        )
    else:
        small = gather_all(far)
        qkv_t = small[:, :, :qkv_part].transpose(1, 2, 0, 3).reshape(3 * width, width)
        mix_t = small[:, :, qkv_part:].transpose(1, 2, 0, 3).reshape(width, width)
        norms = row_spread(jnp.concatenate([norms, router_weight.T.astype(F32)]))
        norms = norms.transpose(1, 0, 2).reshape(4 + E, width)
        router_t = norms[4:].astype(BF16)
        norms = norms[:4]

    routes_t = jnp.pad(
        routes.T.reshape(2, -1, SEQ), ((0, 0), (0, 0), (0, ROWS - SEQ)), constant_values=-1
    ).reshape(2, -1)
    keep_t = jnp.pad(keep.T.reshape(2, -1, SEQ), ((0, 0), (0, 0), (0, ROWS - SEQ))).reshape(2, -1)
    slots = slot_table(routes_t, keep_t)
    columns = slots.T

    sends, laters, saved = attention_forward(here, pieces, cot_pieces, qkv_t, mix_t, norms)
    normed = row_swap(sends)
    others = row_swap(laters)

    def to_experts(x, *earlier):
        return exchange(after(x.reshape(E, CAP, width_part), *earlier))

    x_got = to_experts(dispatch(here, slots, normed), w_got)
    cot_got = to_experts(dispatch(nowhere, slots, [cot]), x_got, *others)
    moved, x_rows, act, slope, res, gates = expert_forward(
        expert, x_got, w_got, router_t, rows, near
    )
    moved = to_experts(moved, cot_got).reshape(E * CAP, width_part)
    grads, grad_pre, grad_res, router_part = expert_backward(
        expert, cot_got, w_got, router_t, x_rows, slope, res, gates, rows, near
    )
    grads = to_experts(grads, moved).reshape(E * CAP, width_part)
    w_grads = expert_grads(x_rows, grad_pre, grad_res, act, w_got, rows, near)
    w_grads = exchange(after(own_experts(w_grads, rows, near, chunks), grads))
    if tiled:
        expert_in_grad, out_grad_t = unpack_grads(w_grads, width_part, hid_part)
    else:
        expert_in_grad = unpack_in(w_grads[:, :out_part], chunks).astype(F32)
        out_grad_t = w_grads[:, out_part:].astype(F32)
    expert_out_grad = out_grad_t.transpose(0, 2, 1)

    back = row_swap(combine(here, columns, grads, rows))
    layer_out = cut_images(finish(here, columns, moved, tok, others))
    back[0] = after(back[0], layer_out)
    sends, outs = attention_backward(
        here, back, pieces, others, qkv_t, mix_t, norms, saved, router_part, half, parts if tiled else None
    )

    if tiled:
        own, other = outs
        got = row_swap(add_core(own, core_swap(other)))
        got = far_swap(add_rows(got))
        qkv_grad, mix_grad, tail = add_far(got, parts)
    else:
        qkv_grad_t, mix_grad_t, tail = outs
        shares = jnp.concatenate(
            [
                qkv_grad_t.reshape(cols, qkv_part, width),
                mix_grad_t.reshape(cols, mix_part, width),
                jnp.broadcast_to(tail[None], (cols,) + tail.shape),
            ],
            axis=1,
        )
        sums = reduce_all(shares)
        qkv_grad, mix_grad, tail = jnp.split(sums, [qkv_part, qkv_part + mix_part])
    thin = width_part // cols
    tail = lax.dynamic_slice_in_dim(tail, col * thin, thin, axis=1)
    tokens_grad = jnp.concatenate(in_order(row_swap(sends), row), axis=0)
    tokens_grad = cut_images(tokens_grad).astype(F32)
    return (
        layer_out,
        tokens_grad,
        tail[E],
        tail[E + 1],
        qkv_grad.T,
        mix_grad.T,
        tail[E + 2],
        tail[E + 3],
        tail[:E].T,
        expert_in_grad,
        expert_out_grad,
    )


def solution(mesh):
    in_specs = (
        P("col", "row"),
        P("row"),
        P("row"),
        P("row", "col"),
        P("row", "col"),
        P("row"),
        P("row"),
        P("row", None),
        P(None, "row", "col"),
        P(None, "row", "col"),
        P("col", None),
        P("col", None),
        P("col", "row"),
    )
    out_specs = (
        P("col", "row"),
        P("col", "row"),
        P(("row", "col")),
        P(("row", "col")),
        P("row", "col"),
        P("row", "col"),
        P(("row", "col")),
        P(("row", "col")),
        P(("row", "col"), None),
        P(None, "row", "col"),
        P(None, "row", "col"),
    )
    return jax.shard_map(local, mesh=mesh, in_specs=in_specs, out_specs=out_specs, check_vma=False)
```

profile of v0, /device:TPU:0, one launch (start us, length us, event | category | flops | bytes accessed | tf_op | source)
XLA Modules:
  0.0 342.4 jit_solution(7111260366642340160)
XLA Ops:
  1.5 3.0 collective-permute-start.3
  4.5 2.6 collective-permute-start.4
  7.1 3.8 %pack_weights.1 = bf16[32,128,512]{2,1,0:T(8,128)(2,1)} custom-call(bf16[32,128,256]{2,1,0:T(8,128)(2,1)} %in_ref.1, bf16[32,64,512]{2,1,0:T(8,128)(2,1)} %bitcast.54), custom_call_target="tpu_custom_call" | custom-call | bytes 8388608 | tf_op jit(solution)/shard_map/pack_weights/pallas_call | solution.py:272
  13.4 4.2 %all-to-all-start = ((bf16[32,128,512]{2,1,0:T(8,128)(2,1)}), bf16[32,128,512]{2,1,0:T(8,128)(2,1)}, u32[]{:S(2)}, u32[]{:S(2)}) async-start(bf16[32,128,512]{2,1,0:T(8,128)(2,1)} %pack_weights.1), calls=%async_computation | async-start | bytes 8388608 | tf_op jit(solution)/shard_map/all_to_all | solution.py:36
  17.5 1.8 collective-permute-start.6
  21.1 35.9 %collective-permute-done.6.refs_1_ = bf16[1072,128]{1,0:T(8,128)(2,1)S(1)} collective-permute-done((bf16[1072,128]{1,0:T(8,128)(2,1)S(1)}, bf16[1072,128]{1,0:T(8,128)(2,1)S(1)}, u32[]{:S(2)}, u32[]{:S(2)}) %collective-permute-start.6) | collective-permute-done | bytes 274464 | tf_op jit(solution)/shard_map/ppermute | solution.py:92
  57.8 8.3 %collective-permute-done.8.refs_3_ = bf16[1072,128]{1,0:T(8,128)(2,1)S(1)} collective-permute-done((bf16[1072,128]{1,0:T(8,128)(2,1)S(1)}, bf16[1072,128]{1,0:T(8,128)(2,1)S(1)}, u32[]{:S(2)}, u32[]{:S(2)}) %collective-permute-start.8) | collective-permute-done | bytes 274464 | tf_op jit(solution)/shard_map/ppermute | solution.py:92
  69.0 2.4 collective-permute-start.2
  72.0 3.4 gather_weights.1
  75.4 3.1 collective-permute-done.1.refs_2_.refs_6_
  79.2 8.5 %attention_forward.1 = (bf16[416,128]{1,0:T(8,128)(2,1)}, bf16[416,128]{1,0:T(8,128)(2,1)}, bf16[416,128]{1,0:T(8,128)(2,1)}, bf16[416,128]{1,0:T(8,128)(2,1)}, ...) custom-call(s32[3]{0:T(128)} %pad_add_fusion.where_ref, ...), custom_call_target="tpu_custom_call" | custom-call | flops 1308622848 | bytes 4194304 | tf_op jit(solution)/shard_map/attention_forward/pallas_call | solution.py:512
  87.7 4.0 %collective-permute-start.13 = (bf16[416,128]{1,0:T(8,128)(2,1)}, bf16[416,128]{1,0:T(8,128)(2,1)S(1)}, u32[]{:S(2)}, u32[]{:S(2)}) collective-permute-start(bf16[416,128]{1,0:T(8,128)(2,1)} %get-tuple-element.75), channel_id=1, source_target_pairs={{0,8},{8,0},{16,24},{24,16},{1,9},{9,1},{17,25},{25,17},{2,10},{10... | collective-permute-start | bytes 319496 | tf_op jit(solution)/shard_map/ppermute | solution.py:92
  94.8 1.6 slots.1.slots_ref
  96.6 1.7 collective-permute-done.14.refs_2_
  99.8 6.9 %dispatch.2 = bf16[3840,128]{1,0:T(8,128)(2,1)} custom-call(s32[3]{0:T(128)} %pad_add_fusion.where_ref, s32[2,1664]{1,0:T(2,128)} %slots.1.slots_ref, bf16[416,128]{1,0:T(8,128)(2,1)} %get-tuple-element.74.refs_0_, bf16[416,128]{1,0:T(8,128)(2,1)} %copy-done.42, bf16[416,128]{1,0:T(8,128)(2,1)} %copy-done.43, bf16[416,128]{1,0:T(8,128)(2,1)} %copy-done.44), custom_call_target="tpu_custom_call" | custom-call | flops 1635778560 | bytes 1409024 | tf_op jit(solution)/shard_map/dispatch/pallas_call | solution.py:356
  106.7 5.9 %all-to-all-done.w_ref = bf16[32,128,512]{2,1,0:T(8,128)(2,1)} async-done(((bf16[32,128,512]{2,1,0:T(8,128)(2,1)}), bf16[32,128,512]{2,1,0:T(8,128)(2,1)}, u32[]{:S(2)}, u32[]{:S(2)}) %all-to-all-start) | async-done | bytes 4194336 | tf_op jit(solution)/shard_map/all_to_all | solution.py:36
  112.6 2.6 all-to-all-start.1
  115.3 1.7 collective-permute-start.16
  118.8 6.8 %dispatch.3 = bf16[3840,128]{1,0:T(8,128)(2,1)} custom-call(s32[1]{0:T(128)} %constant.72.clone.1.where_ref, s32[2,1664]{1,0:T(2,128)} %slots.1.slots_ref, bf16[1664,128]{1,0:T(8,128)(2,1)} %bitcast.58), custom_call_target="tpu_custom_call" | custom-call | flops 1635778560 | bytes 1409024 | tf_op jit(solution)/shard_map/dispatch/pallas_call | solution.py:356
  125.6 5.3 %collective-permute-done.16.refs_1_.refs_9_ = bf16[2,416,128]{2,1,0:T(8,128)(2,1)S(1)} collective-permute-done((bf16[2,416,128]{2,1,0:T(8,128)(2,1)S(1)}, bf16[2,416,128]{2,1,0:T(8,128)(2,1)S(1)}, u32[]{:S(2)}, u32[]{:S(2)}) %collective-permute-start.16) | collective-permute-done | bytes 213024 | tf_op jit(solution)/shard_map/ppermute | solution.py:92
  130.9 7.4 %collective-permute-done.18.refs_3_.refs_11_ = bf16[2,416,128]{2,1,0:T(8,128)(2,1)S(1)} collective-permute-done((bf16[2,416,128]{2,1,0:T(8,128)(2,1)S(1)}, bf16[2,416,128]{2,1,0:T(8,128)(2,1)S(1)}, u32[]{:S(2)}, u32[]{:S(2)}) %collective-permute-start.18) | collective-permute-done | bytes 213024 | tf_op jit(solution)/shard_map/ppermute | solution.py:92
  138.3 3.2 all-to-all-done.1.got_ref
  141.4 2.6 all-to-all-start.2
  144.1 18.4 %expert_forward.1 = (bf16[32,120,128]{2,1,0:T(8,128)(2,1)}, bf16[960,512]{1,0:T(8,128)(2,1)}, bf16[4,960,512]{2,1,0:T(8,128)(2,1)}, bf16[4,960,512]{2,1,0:T(8,12...) custom-call(s32[1]{0:T(128)} %bitcast.6.e_ref, bf16[32,120,128]{2,1,0:T(8,128)(2,1)} %copy-done.4, ...), custom_call_target="tpu_custom_call" | custom-call | flops 4026531840 | bytes 16777216 | tf_op jit(solution)/shard_map/expert_forward/pallas_call | solution.py:860
  162.5 7.7 %all-to-all-done.2.got_ref = bf16[32,120,128]{2,1,0:T(8,128)(2,1)S(1)} async-done(((bf16[32,120,128]{2,1,0:T(8,128)(2,1)}), bf16[32,120,128]{2,1,0:T(8,128)(2,1)S(1)}, u32[]{:S(2)}, u32[]{:S(2)}) %all-to-all-start.2) | async-done | bytes 983072 | tf_op jit(solution)/shard_map/all_to_all | solution.py:36
  170.3 2.6 all-to-all-start.3
  172.9 12.4 %expert_backward.1 = (bf16[32,120,128]{2,1,0:T(8,128)(2,1)}, bf16[4,960,512]{2,1,0:T(8,128)(2,1)}, bf16[960,512]{1,0:T(8,128)(2,1)}, f32[32,512]{1,0:T(8,128)}) custom-call(s32[1]{0:T(128)} %bitcast.6.e_ref, bf16[32,120,128]{2,1,0:T(8,128)(2,1)} %copy-done.6, bf16[32,128,512]{2,1,0:T(8,128)(2,1)} %all-to-all-done.w_ref, ...), custom_call_target="tpu_custom_call" | custom-call | flops 4026531840 | bytes 16777216 | tf_op jit(solution)/shard_map/expert_backward/pallas_call | solution.py:909
  185.3 13.8 %all-to-all-done.3 = bf16[32,120,128]{2,1,0:T(8,128)(2,1)S(1)} async-done(((bf16[32,120,128]{2,1,0:T(8,128)(2,1)}), bf16[32,120,128]{2,1,0:T(8,128)(2,1)S(1)}, u32[]{:S(2)}, u32[]{:S(2)}) %all-to-all-start.3) | async-done | bytes 983072 | tf_op jit(solution)/shard_map/all_to_all | solution.py:36
  199.1 2.6 all-to-all-start.4
  201.7 11.1 %expert_grads.1 = bf16[32,128,512]{2,1,0:T(8,128)(2,1)} custom-call(bf16[960,512]{1,0:T(8,128)(2,1)} %get-tuple-element.88.x_ref, bf16[4,960,512]{2,1,0:T(8,128)(2,1)} %get-tuple-element.121.pre_ref, bf16[960,512]{1,0:T(8,128)(2,1)} %get-tuple-element.122.grad_res_ref, bf16[4,960,512]{2,1,0:T(8,128)(2,1)} %get-tuple-element.123.act_ref), custom_call_target="tpu_custom_call" | custom-call | flops 4026531840 | bytes 16777216 | tf_op jit(solution)/shard_map/expert_grads/pallas_call | solution.py:951
  212.8 15.1 %all-to-all-done.4 = bf16[32,120,128]{2,1,0:T(8,128)(2,1)S(1)} async-done(((bf16[32,120,128]{2,1,0:T(8,128)(2,1)}), bf16[32,120,128]{2,1,0:T(8,128)(2,1)S(1)}, u32[]{:S(2)}, u32[]{:S(2)}) %all-to-all-start.4) | async-done | bytes 983072 | tf_op jit(solution)/shard_map/all_to_all | solution.py:36
  228.9 3.8 %all-to-all-start.5 = ((bf16[32,128,512]{2,1,0:T(8,128)(2,1)}), bf16[32,128,512]{2,1,0:T(8,128)(2,1)}, u32[]{:S(2)}, u32[]{:S(2)}) async-start(bf16[32,128,512]{2,1,0:T(8,128)(2,1)} %expert_grads.1), calls=%async_computation.5 | async-start | bytes 8388608 | tf_op jit(solution)/shard_map/all_to_all | solution.py:36
  233.9 7.3 %combine.1 = (bf16[416,128]{1,0:T(8,128)(2,1)}, bf16[416,128]{1,0:T(8,128)(2,1)}, bf16[416,128]{1,0:T(8,128)(2,1)}, bf16[416,128]{1,0:T(8,128)(2,1)}) custom-call(s32[3]{0:T(128)} %pad_add_fusion.where_ref, s32[1664,2]{1,0:T(8,128)} %bitcast.64, bf16[3840,128]{1,0:T(8,128)(2,1)} %bitcast.63), custom_call_target="tpu_custom_call" | custom-call | flops 1635778560 | bytes 1409024 | tf_op jit(solution)/shard_map/combine/pallas_call | solution.py:390
  244.7 7.8 %finish.1 = bf16[1664,128]{1,0:T(8,128)(2,1)} custom-call(s32[3]{0:T(128)} %pad_add_fusion.where_ref, s32[1664,2]{1,0:T(8,128)} %bitcast.65, bf16[3840,128]{1,0:T(8,128)(2,1)} %bitcast.60, bf16[1664,128]{1,0:T(8,128)(2,1)} %bitcast.56, bf16[2,416,128]{2,1,0:T(8,128)(2,1)} %get-tuple-element.82.refs_0_.refs_8_, bf16[2,416,128]{2,1,0:T(8,128)(2,1)} %copy-done.31, ...), custom_call_target="tpu_custom_call" | custom-call | flops 1635778560 | bytes 2260992 | tf_op jit(solution)/shard_map/finish/pallas_call | solution.py:419
  254.4 9.0 %collective-permute-done.19.refs_1_ = bf16[416,128]{1,0:T(8,128)(2,1)S(1)} collective-permute-done((bf16[416,128]{1,0:T(8,128)(2,1)}, bf16[416,128]{1,0:T(8,128)(2,1)S(1)}, u32[]{:S(2)}, u32[]{:S(2)}) %collective-permute-start.19) | collective-permute-done | bytes 106528 | tf_op jit(solution)/shard_map/ppermute | solution.py:92
  263.4 7.1 %collective-permute-done.21.refs_3_ = bf16[416,128]{1,0:T(8,128)(2,1)S(1)} collective-permute-done((bf16[416,128]{1,0:T(8,128)(2,1)}, bf16[416,128]{1,0:T(8,128)(2,1)S(1)}, u32[]{:S(2)}, u32[]{:S(2)}) %collective-permute-start.21) | collective-permute-done | bytes 106528 | tf_op jit(solution)/shard_map/ppermute | solution.py:92
  271.2 15.7 %attention_backward.1 = (bf16[416,128]{1,0:T(8,128)(2,1)}, bf16[416,128]{1,0:T(8,128)(2,1)}, bf16[416,128]{1,0:T(8,128)(2,1)}, bf16[416,128]{1,0:T(8,128)(2,1)},...) custom-call(s32[3]{0:T(128)} %pad_add_fusion.where_ref, bf16[416,128]{1,0:T(8,128)(2,1)} %get-tuple-element.95.refs_0_, ...), custom_call_target="tpu_custom_call" | custom-call | flops 3271557120 | bytes 8388608 | tf_op jit(solution)/shard_map/attention_backward/pallas_call | solution.py:664
  287.8 2.7 collective-permute-start.24
  291.6 2.8 add_core.1
  295.0 2.5 collective-permute-done.22
  300.0 8.5 %collective-permute-done.26.refs_1_ = bf16[4,304,128]{2,1,0:T(8,128)(2,1)S(1)} collective-permute-done((bf16[4,304,128]{2,1,0:T(8,128)(2,1)}, bf16[4,304,128]{2,1,0:T(8,128)(2,1)S(1)}, u32[]{:S(2)}, u32[]{:S(2)}) %collective-permute-start.26) | collective-permute-done | bytes 311328 | tf_op jit(solution)/shard_map/ppermute | solution.py:92
  308.5 9.0 %collective-permute-done.28.refs_3_ = bf16[4,304,128]{2,1,0:T(8,128)(2,1)S(1)} collective-permute-done((bf16[4,304,128]{2,1,0:T(8,128)(2,1)}, bf16[4,304,128]{2,1,0:T(8,128)(2,1)S(1)}, u32[]{:S(2)}, u32[]{:S(2)}) %collective-permute-start.28) | collective-permute-done | bytes 311328 | tf_op jit(solution)/shard_map/ppermute | solution.py:92
  318.2 2.0 add_rows.1
  320.2 3.5 %collective-permute-start.29 = (bf16[304,128]{1,0:T(8,128)(2,1)}, bf16[304,128]{1,0:T(8,128)(2,1)S(1)}, u32[]{:S(2)}, u32[]{:S(2)}) collective-permute-start(bf16[304,128]{1,0:T(8,128)(2,1)} %get-tuple-element.115), channel_id=1, source_target_pairs={{0,2},{1,3},{2,0},{3,1},{4,6},{5,7},{6,4},{7,5},{8,10},{9,11},{10,... | collective-permute-start | bytes 233480 | tf_op jit(solution)/shard_map/ppermute | solution.py:107
  327.1 1.5 collective-permute-done.29.refs_1_
  328.6 3.4 %collective-permute-done.30.refs_2_ = bf16[304,128]{1,0:T(8,128)(2,1)S(1)} collective-permute-done((bf16[304,128]{1,0:T(8,128)(2,1)}, bf16[304,128]{1,0:T(8,128)(2,1)S(1)}, u32[]{:S(2)}, u32[]{:S(2)}) %collective-permute-start.30) | collective-permute-done | bytes 77856 | tf_op jit(solution)/shard_map/ppermute | solution.py:107
  332.7 1.7 add_far.1
  337.3 5.1 %unpack_grads.1 = (f32[32,128,256]{2,1,0:T(8,128)}, f32[32,64,512]{2,1,0:T(8,128)}) custom-call(bf16[32,128,512]{2,1,0:T(8,128)(2,1)} %all-to-all-done.5.got_ref), custom_call_target="tpu_custom_call" | custom-call | bytes 12582912 | tf_op jit(solution)/shard_map/unpack_grads/pallas_call | solution.py:289
  (161 shorter events, 37.5 us)
Async XLA Ops:
  1.5 9.5 %collective-permute-start.3 = (bf16[256,128]{1,0:T(8,128)(2,1)S(1)}, bf16[256,128]{1,0:T(8,128)(2,1)S(1)}, u32[]{:S(2)}, u32[]{:S(2)}) collective-permute-start(bf16[256,128]{1,0:T(8,128)(2,1)S(1)} %pad_maximum_fusion.1), channel_id=1, source_target_pairs={{0,2},{1,3},{2,0},{3,1},{4,6},{5,7},{6,4},{7,5},{8,10},{9,11},{10,... | collective-permute-start | bytes 196616 | tf_op jit(solution)/shard_map/ppermute | solution.py:107
  4.5 7.3 %collective-permute-start.4 = (bf16[256,128]{1,0:T(8,128)(2,1)S(1)}, bf16[256,128]{1,0:T(8,128)(2,1)S(1)}, u32[]{:S(2)}, u32[]{:S(2)}) collective-permute-start(bf16[256,128]{1,0:T(8,128)(2,1)S(1)} %pad_maximum_fusion.1), channel_id=1, source_target_pairs={{0,4},{1,5},{2,6},{3,7},{4,0},{5,1},{6,2},{7,3},{8,12},{9,13},{10,... | collective-permute-start | bytes 196616 | tf_op jit(solution)/shard_map/ppermute | solution.py:107
  7.1 6.1 %collective-permute-start.5 = (bf16[256,128]{1,0:T(8,128)(2,1)S(1)}, bf16[256,128]{1,0:T(8,128)(2,1)S(1)}, u32[]{:S(2)}, u32[]{:S(2)}) collective-permute-start(bf16[256,128]{1,0:T(8,128)(2,1)S(1)} %pad_maximum_fusion.1), channel_id=1, source_target_pairs={{0,6},{1,7},{2,4},{3,5},{4,2},{5,3},{6,0},{7,1},{8,14},{9,15},{10,... | collective-permute-start | bytes 196616 | tf_op jit(solution)/shard_map/ppermute | solution.py:107
  13.3 43.7 %copy-start.8 = (bf16[1576,128]{1,0:T(8,128)(2,1)S(1)}, bf16[1576,128]{1,0:T(8,128)(2,1)}, u32[]{:S(2)}) copy-start(bf16[1576,128]{1,0:T(8,128)(2,1)} %param.13) | copy-start | bytes 1210372
  13.3 53.9 %copy-start.9 = (bf16[1576,128]{1,0:T(8,128)(2,1)S(1)}, bf16[1576,128]{1,0:T(8,128)(2,1)}, u32[]{:S(2)}) copy-start(bf16[1576,128]{1,0:T(8,128)(2,1)} %param.25) | copy-start | bytes 1210372
  13.4 99.2 %all-to-all-start = ((bf16[32,128,512]{2,1,0:T(8,128)(2,1)}), bf16[32,128,512]{2,1,0:T(8,128)(2,1)}, u32[]{:S(2)}, u32[]{:S(2)}) async-start(bf16[32,128,512]{2,1,0:T(8,128)(2,1)} %pack_weights.1), calls=%async_computation | async-start | bytes 8388608 | tf_op jit(solution)/shard_map/all_to_all | solution.py:36
  17.5 39.5 %collective-permute-start.6 = (bf16[1072,128]{1,0:T(8,128)(2,1)S(1)}, bf16[1072,128]{1,0:T(8,128)(2,1)S(1)}, u32[]{:S(2)}, u32[]{:S(2)}) collective-permute-start(bf16[1072,128]{1,0:T(8,128)(2,1)S(1)} %concatenate.11.refs_0_), channel_id=1, source_target_pairs={{0,8},{8,0},{16,24},{24,16},{1,9},{9,1},{17,25},{25,17},{2,10},{10... | collective-permute-start | bytes 823304 | tf_op jit(solution)/shard_map/ppermute | solution.py:92
  19.3 37.9 %collective-permute-start.7 = (bf16[1072,128]{1,0:T(8,128)(2,1)S(1)}, bf16[1072,128]{1,0:T(8,128)(2,1)S(1)}, u32[]{:S(2)}, u32[]{:S(2)}) collective-permute-start(bf16[1072,128]{1,0:T(8,128)(2,1)S(1)} %concatenate.11.refs_0_), channel_id=1, source_target_pairs={{0,16},{8,24},{16,0},{24,8},{1,17},{9,25},{17,1},{25,9},{2,18},{10... | collective-permute-start | bytes 823304 | tf_op jit(solution)/shard_map/ppermute | solution.py:92
  20.8 45.3 %collective-permute-start.8 = (bf16[1072,128]{1,0:T(8,128)(2,1)S(1)}, bf16[1072,128]{1,0:T(8,128)(2,1)S(1)}, u32[]{:S(2)}, u32[]{:S(2)}) collective-permute-start(bf16[1072,128]{1,0:T(8,128)(2,1)S(1)} %concatenate.11.refs_0_), channel_id=1, source_target_pairs={{0,24},{8,16},{16,8},{24,0},{1,25},{9,17},{17,9},{25,1},{2,26},{10... | collective-permute-start | bytes 823304 | tf_op jit(solution)/shard_map/ppermute | solution.py:92
  21.1 47.2 %collective-permute-start.9 = (bf16[1072,128]{1,0:T(8,128)(2,1)S(1)}, bf16[1072,128]{1,0:T(8,128)(2,1)S(1)}, u32[]{:S(2)}, u32[]{:S(2)}) collective-permute-start(bf16[1072,128]{1,0:T(8,128)(2,1)S(1)} %concatenate.11.refs_0_), channel_id=1, source_target_pairs={{0,1},{1,0},{2,3},{3,2},{4,5},{5,4},{6,7},{7,6},{8,9},{9,8},{10,11... | collective-permute-start | bytes 823304 | tf_op jit(solution)/shard_map/ppermute | solution.py:112
  57.0 12.0 %collective-permute-start.10 = (bf16[1072,128]{1,0:T(8,128)(2,1)S(1)}, bf16[1072,128]{1,0:T(8,128)(2,1)S(1)}, u32[]{:S(2)}, u32[]{:S(2)}) collective-permute-start(bf16[1072,128]{1,0:T(8,128)(2,1)S(1)} %collective-permute-done.6.refs_1_), channel_id=1, source_target_pairs={{0,1},{1,0},{2,3},{3,2},{4,5},{5,4},{6,7},{7,6},{8,9},{9,8},{10,11... | collective-permute-start | bytes 823304 | tf_op jit(solution)/shard_map/ppermute | solution.py:112
  57.2 30.5 %copy-start = (bf16[8,208,128]{2,1,0:T(8,128)(2,1)}, bf16[8,208,128]{2,1,0:T(8,128)(2,1)S(1)}, u32[]{:S(2)}) copy-start(bf16[8,208,128]{2,1,0:T(8,128)(2,1)S(1)} %pad.16) | copy-start | bytes 1277956
  57.2 14.7 %collective-permute-start.11 = (bf16[1072,128]{1,0:T(8,128)(2,1)S(1)}, bf16[1072,128]{1,0:T(8,128)(2,1)}, u32[]{:S(2)}, u32[]{:S(2)}) collective-permute-start(bf16[1072,128]{1,0:T(8,128)(2,1)S(1)} %collective-permute-done.7.refs_2_), channel_id=1, source_target_pairs={{0,1},{1,0},{2,3},{3,2},{4,5},{5,4},{6,7},{7,6},{8,9},{9,8},{10,11... | collective-permute-start | bytes 823304 | tf_op jit(solution)/shard_map/ppermute | solution.py:112
  66.1 5.9 %collective-permute-start.12 = (bf16[1072,128]{1,0:T(8,128)(2,1)S(1)}, bf16[1072,128]{1,0:T(8,128)(2,1)}, u32[]{:S(2)}, u32[]{:S(2)}) collective-permute-start(bf16[1072,128]{1,0:T(8,128)(2,1)S(1)} %collective-permute-done.8.refs_3_), channel_id=1, source_target_pairs={{0,1},{1,0},{2,3},{3,2},{4,5},{5,4},{6,7},{7,6},{8,9},{9,8},{10,11... | collective-permute-start | bytes 823304 | tf_op jit(solution)/shard_map/ppermute | solution.py:112
  66.8 8.5 %collective-permute-start = (bf16[416,128]{1,0:T(8,128)(2,1)}, bf16[416,128]{1,0:T(8,128)(2,1)}, u32[]{:S(2)}, u32[]{:S(2)}) collective-permute-start(bf16[416,128]{1,0:T(8,128)(2,1)} %get-tuple-element.159), channel_id=1, source_target_pairs={{0,8},{8,0},{16,24},{24,16},{1,9},{9,1},{17,25},{25,17},{2,10},{10... | collective-permute-start | bytes 319496 | tf_op jit(solution)/shard_map/ppermute | solution.py:92
  67.4 20.2 %copy-start.1 = (bf16[8,208,128]{2,1,0:T(8,128)(2,1)}, bf16[8,208,128]{2,1,0:T(8,128)(2,1)S(1)}, u32[]{:S(2)}) copy-start(bf16[8,208,128]{2,1,0:T(8,128)(2,1)S(1)} %pad.17) | copy-start | bytes 1277956
  67.5 25.7 %copy-start.24 = (s32[1576,2]{0,1:T(2,128)S(1)}, s32[1576,2]{0,1:T(2,128)}, u32[]{:S(2)}) copy-start(s32[1576,2]{0,1:T(2,128)} %param.23) | copy-start | bytes 37828
  67.5 26.5 %copy-start.25 = (s32[1576,2]{0,1:T(2,128)S(1)}, s32[1576,2]{0,1:T(2,128)}, u32[]{:S(2)}) copy-start(s32[1576,2]{0,1:T(2,128)} %param.24) | copy-start | bytes 37828
  68.3 10.2 %collective-permute-start.1 = (bf16[416,128]{1,0:T(8,128)(2,1)S(1)}, bf16[416,128]{1,0:T(8,128)(2,1)S(1)}, u32[]{:S(2)}, u32[]{:S(2)}) collective-permute-start(bf16[416,128]{1,0:T(8,128)(2,1)S(1)} %get-tuple-element.158), channel_id=1, source_target_pairs={{0,16},{8,24},{16,0},{24,8},{1,17},{9,25},{17,1},{25,9},{2,18},{10... | collective-permute-start | bytes 319496 | tf_op jit(solution)/shard_map/ppermute | solution.py:92
  69.0 9.5 %collective-permute-start.2 = (bf16[416,128]{1,0:T(8,128)(2,1)S(1)}, bf16[416,128]{1,0:T(8,128)(2,1)S(1)}, u32[]{:S(2)}, u32[]{:S(2)}) collective-permute-start(bf16[416,128]{1,0:T(8,128)(2,1)S(1)} %get-tuple-element.157), channel_id=1, source_target_pairs={{0,24},{8,16},{16,8},{24,0},{1,25},{9,17},{17,9},{25,1},{2,26},{10... | collective-permute-start | bytes 319496 | tf_op jit(solution)/shard_map/ppermute | solution.py:92
  87.7 8.9 %collective-permute-start.13 = (bf16[416,128]{1,0:T(8,128)(2,1)}, bf16[416,128]{1,0:T(8,128)(2,1)S(1)}, u32[]{:S(2)}, u32[]{:S(2)}) collective-permute-start(bf16[416,128]{1,0:T(8,128)(2,1)} %get-tuple-element.75), channel_id=1, source_target_pairs={{0,8},{8,0},{16,24},{24,16},{1,9},{9,1},{17,25},{25,17},{2,10},{10... | collective-permute-start | bytes 319496 | tf_op jit(solution)/shard_map/ppermute | solution.py:92
  91.7 6.6 %collective-permute-start.14 = (bf16[416,128]{1,0:T(8,128)(2,1)}, bf16[416,128]{1,0:T(8,128)(2,1)S(1)}, u32[]{:S(2)}, u32[]{:S(2)}) collective-permute-start(bf16[416,128]{1,0:T(8,128)(2,1)} %get-tuple-element.76), channel_id=1, source_target_pairs={{0,16},{8,24},{16,0},{24,8},{1,17},{9,25},{17,1},{25,9},{2,18},{10... | collective-permute-start | bytes 319496 | tf_op jit(solution)/shard_map/ppermute | solution.py:92
  92.2 7.0 %collective-permute-start.15 = (bf16[416,128]{1,0:T(8,128)(2,1)}, bf16[416,128]{1,0:T(8,128)(2,1)S(1)}, u32[]{:S(2)}, u32[]{:S(2)}) collective-permute-start(bf16[416,128]{1,0:T(8,128)(2,1)} %get-tuple-element.77), channel_id=1, source_target_pairs={{0,24},{8,16},{16,8},{24,0},{1,25},{9,17},{17,9},{25,1},{2,26},{10... | collective-permute-start | bytes 319496 | tf_op jit(solution)/shard_map/ppermute | solution.py:92
  99.8 18.6 %copy-start.34 = (bf16[2,416,128]{2,1,0:T(8,128)(2,1)S(1)}, bf16[2,416,128]{2,1,0:T(8,128)(2,1)}, u32[]{:S(2)}) copy-start(bf16[2,416,128]{2,1,0:T(8,128)(2,1)} %get-tuple-element.85) | copy-start | bytes 638980
  112.6 28.8 %all-to-all-start.1 = ((bf16[32,120,128]{2,1,0:T(8,128)(2,1)}), bf16[32,120,128]{2,1,0:T(8,128)(2,1)S(1)}, u32[]{:S(2)}, u32[]{:S(2)}) async-start(bf16[32,120,128]{2,1,0:T(8,128)(2,1)} %bitcast.62), calls=%async_computation.1 | async-start | bytes 1966080 | tf_op jit(solution)/shard_map/all_to_all | solution.py:36
  115.3 15.6 %collective-permute-start.16 = (bf16[2,416,128]{2,1,0:T(8,128)(2,1)S(1)}, bf16[2,416,128]{2,1,0:T(8,128)(2,1)S(1)}, u32[]{:S(2)}, u32[]{:S(2)}) collective-permute-start(bf16[2,416,128]{2,1,0:T(8,128)(2,1)S(1)} %copy-done.36), channel_id=1, source_target_pairs={{0,8},{8,0},{16,24},{24,16},{1,9},{9,1},{17,25},{25,17},{2,10},{10... | collective-permute-start | bytes 638984 | tf_op jit(solution)/shard_map/ppermute | solution.py:92
  117.0 13.9 %collective-permute-start.17 = (bf16[2,416,128]{2,1,0:T(8,128)(2,1)S(1)}, bf16[2,416,128]{2,1,0:T(8,128)(2,1)S(1)}, u32[]{:S(2)}, u32[]{:S(2)}) collective-permute-start(bf16[2,416,128]{2,1,0:T(8,128)(2,1)S(1)} %copy-done.35), channel_id=1, source_target_pairs={{0,16},{8,24},{16,0},{24,8},{1,17},{9,25},{17,1},{25,9},{2,18},{10... | collective-permute-start | bytes 638984 | tf_op jit(solution)/shard_map/ppermute | solution.py:92
  118.5 19.8 %collective-permute-start.18 = (bf16[2,416,128]{2,1,0:T(8,128)(2,1)S(1)}, bf16[2,416,128]{2,1,0:T(8,128)(2,1)S(1)}, u32[]{:S(2)}, u32[]{:S(2)}) collective-permute-start(bf16[2,416,128]{2,1,0:T(8,128)(2,1)S(1)} %copy-done.34), channel_id=1, source_target_pairs={{0,24},{8,16},{16,8},{24,0},{1,25},{9,17},{17,9},{25,1},{2,26},{10... | collective-permute-start | bytes 638984 | tf_op jit(solution)/shard_map/ppermute | solution.py:92
  130.9 31.6 %copy-start.31 = (bf16[2,416,128]{2,1,0:T(8,128)(2,1)}, bf16[2,416,128]{2,1,0:T(8,128)(2,1)S(1)}, u32[]{:S(2)}) copy-start(bf16[2,416,128]{2,1,0:T(8,128)(2,1)S(1)} %collective-permute-done.16.refs_1_.refs_9_) | copy-start | bytes 638980
  130.9 31.6 %copy-start.32 = (bf16[2,416,128]{2,1,0:T(8,128)(2,1)}, bf16[2,416,128]{2,1,0:T(8,128)(2,1)S(1)}, u32[]{:S(2)}) copy-start(bf16[2,416,128]{2,1,0:T(8,128)(2,1)S(1)} %collective-permute-done.17.refs_2_.refs_10_) | copy-start | bytes 638980
  138.3 24.3 %copy-start.33 = (bf16[2,416,128]{2,1,0:T(8,128)(2,1)}, bf16[2,416,128]{2,1,0:T(8,128)(2,1)S(1)}, u32[]{:S(2)}) copy-start(bf16[2,416,128]{2,1,0:T(8,128)(2,1)S(1)} %collective-permute-done.18.refs_3_.refs_11_) | copy-start | bytes 638980
  141.4 28.8 %all-to-all-start.2 = ((bf16[32,120,128]{2,1,0:T(8,128)(2,1)}), bf16[32,120,128]{2,1,0:T(8,128)(2,1)S(1)}, u32[]{:S(2)}, u32[]{:S(2)}) async-start(bf16[32,120,128]{2,1,0:T(8,128)(2,1)} %bitcast.61), calls=%async_computation.2 | async-start | bytes 1966080 | tf_op jit(solution)/shard_map/all_to_all | solution.py:36
  170.3 28.8 %all-to-all-start.3 = ((bf16[32,120,128]{2,1,0:T(8,128)(2,1)}), bf16[32,120,128]{2,1,0:T(8,128)(2,1)S(1)}, u32[]{:S(2)}, u32[]{:S(2)}) async-start(bf16[32,120,128]{2,1,0:T(8,128)(2,1)} %get-tuple-element.87), calls=%async_computation.3 | async-start | bytes 1966080 | tf_op jit(solution)/shard_map/all_to_all | solution.py:36
  199.1 28.8 %all-to-all-start.4 = ((bf16[32,120,128]{2,1,0:T(8,128)(2,1)}), bf16[32,120,128]{2,1,0:T(8,128)(2,1)S(1)}, u32[]{:S(2)}, u32[]{:S(2)}) async-start(bf16[32,120,128]{2,1,0:T(8,128)(2,1)} %get-tuple-element.93), calls=%async_computation.4 | async-start | bytes 1966080 | tf_op jit(solution)/shard_map/all_to_all | solution.py:36
  228.9 108.4 %all-to-all-start.5 = ((bf16[32,128,512]{2,1,0:T(8,128)(2,1)}), bf16[32,128,512]{2,1,0:T(8,128)(2,1)}, u32[]{:S(2)}, u32[]{:S(2)}) async-start(bf16[32,128,512]{2,1,0:T(8,128)(2,1)} %expert_grads.1), calls=%async_computation.5 | async-start | bytes 8388608 | tf_op jit(solution)/shard_map/all_to_all | solution.py:36
  241.2 22.2 %collective-permute-start.19 = (bf16[416,128]{1,0:T(8,128)(2,1)}, bf16[416,128]{1,0:T(8,128)(2,1)S(1)}, u32[]{:S(2)}, u32[]{:S(2)}) collective-permute-start(bf16[416,128]{1,0:T(8,128)(2,1)} %get-tuple-element.96), channel_id=1, source_target_pairs={{0,8},{8,0},{16,24},{24,16},{1,9},{9,1},{17,25},{25,17},{2,10},{10... | collective-permute-start | bytes 319496 | tf_op jit(solution)/shard_map/ppermute | solution.py:92
  242.6 20.8 %collective-permute-start.20 = (bf16[416,128]{1,0:T(8,128)(2,1)}, bf16[416,128]{1,0:T(8,128)(2,1)S(1)}, u32[]{:S(2)}, u32[]{:S(2)}) collective-permute-start(bf16[416,128]{1,0:T(8,128)(2,1)} %get-tuple-element.97), channel_id=1, source_target_pairs={{0,16},{8,24},{16,0},{24,8},{1,17},{9,25},{17,1},{25,9},{2,18},{10... | collective-permute-start | bytes 319496 | tf_op jit(solution)/shard_map/ppermute | solution.py:92
  244.1 26.4 %collective-permute-start.21 = (bf16[416,128]{1,0:T(8,128)(2,1)}, bf16[416,128]{1,0:T(8,128)(2,1)S(1)}, u32[]{:S(2)}, u32[]{:S(2)}) collective-permute-start(bf16[416,128]{1,0:T(8,128)(2,1)} %get-tuple-element.98), channel_id=1, source_target_pairs={{0,24},{8,16},{16,8},{24,0},{1,25},{9,17},{17,9},{25,1},{2,26},{10... | collective-permute-start | bytes 319496 | tf_op jit(solution)/shard_map/ppermute | solution.py:92
  286.9 3.6 %collective-permute-start.25 = (bf16[4,4,304,128]{3,2,1,0:T(8,128)(2,1)}, bf16[4,4,304,128]{3,2,1,0:T(8,128)(2,1)S(1)}, u32[]{:S(2)}, u32[]{:S(2)}) collective-permute-start(bf16[4,4,304,128]{3,2,1,0:T(8,128)(2,1)} %get-tuple-element.109), channel_id=1, source_target_pairs={{0,1},{1,0},{2,3},{3,2},{4,5},{5,4},{6,7},{7,6},{8,9},{9,8},{10,11... | collective-permute-start | bytes 3735560 | tf_op jit(solution)/shard_map/ppermute | solution.py:112
  287.0 10.6 %collective-permute-start.22 = (bf16[416,128]{1,0:T(8,128)(2,1)}, bf16[416,128]{1,0:T(8,128)(2,1)S(1)}, u32[]{:S(2)}, u32[]{:S(2)}) collective-permute-start(bf16[416,128]{1,0:T(8,128)(2,1)} %get-tuple-element.104), channel_id=1, source_target_pairs={{0,24},{8,16},{16,8},{24,0},{1,25},{9,17},{17,9},{25,1},{2,26},{10... | collective-permute-start | bytes 319496 | tf_op jit(solution)/shard_map/ppermute | solution.py:92
  287.0 11.1 %collective-permute-start.23 = (bf16[416,128]{1,0:T(8,128)(2,1)}, bf16[416,128]{1,0:T(8,128)(2,1)S(1)}, u32[]{:S(2)}, u32[]{:S(2)}) collective-permute-start(bf16[416,128]{1,0:T(8,128)(2,1)} %get-tuple-element.105), channel_id=1, source_target_pairs={{0,16},{8,24},{16,0},{24,8},{1,17},{9,25},{17,1},{25,9},{2,18},{10... | collective-permute-start | bytes 319496 | tf_op jit(solution)/shard_map/ppermute | solution.py:92
  287.8 11.2 %collective-permute-start.24 = (bf16[416,128]{1,0:T(8,128)(2,1)}, bf16[416,128]{1,0:T(8,128)(2,1)S(1)}, u32[]{:S(2)}, u32[]{:S(2)}) collective-permute-start(bf16[416,128]{1,0:T(8,128)(2,1)} %get-tuple-element.106), channel_id=1, source_target_pairs={{0,8},{8,0},{16,24},{24,16},{1,9},{9,1},{17,25},{25,17},{2,10},{10... | collective-permute-start | bytes 319496 | tf_op jit(solution)/shard_map/ppermute | solution.py:92
  294.3 14.1 %collective-permute-start.26 = (bf16[4,304,128]{2,1,0:T(8,128)(2,1)}, bf16[4,304,128]{2,1,0:T(8,128)(2,1)S(1)}, u32[]{:S(2)}, u32[]{:S(2)}) collective-permute-start(bf16[4,304,128]{2,1,0:T(8,128)(2,1)} %get-tuple-element.111), channel_id=1, source_target_pairs={{0,8},{8,0},{16,24},{24,16},{1,9},{9,1},{17,25},{25,17},{2,10},{10... | collective-permute-start | bytes 933896 | tf_op jit(solution)/shard_map/ppermute | solution.py:92
  294.3 14.1 %collective-permute-start.27 = (bf16[4,304,128]{2,1,0:T(8,128)(2,1)}, bf16[4,304,128]{2,1,0:T(8,128)(2,1)S(1)}, u32[]{:S(2)}, u32[]{:S(2)}) collective-permute-start(bf16[4,304,128]{2,1,0:T(8,128)(2,1)} %get-tuple-element.112), channel_id=1, source_target_pairs={{0,16},{8,24},{16,0},{24,8},{1,17},{9,25},{17,1},{25,9},{2,18},{10... | collective-permute-start | bytes 933896 | tf_op jit(solution)/shard_map/ppermute | solution.py:92
  297.5 19.9 %collective-permute-start.28 = (bf16[4,304,128]{2,1,0:T(8,128)(2,1)}, bf16[4,304,128]{2,1,0:T(8,128)(2,1)S(1)}, u32[]{:S(2)}, u32[]{:S(2)}) collective-permute-start(bf16[4,304,128]{2,1,0:T(8,128)(2,1)} %get-tuple-element.113), channel_id=1, source_target_pairs={{0,24},{8,16},{16,8},{24,0},{1,25},{9,17},{17,9},{25,1},{2,26},{10... | collective-permute-start | bytes 933896 | tf_op jit(solution)/shard_map/ppermute | solution.py:92
  320.2 8.4 %collective-permute-start.29 = (bf16[304,128]{1,0:T(8,128)(2,1)}, bf16[304,128]{1,0:T(8,128)(2,1)S(1)}, u32[]{:S(2)}, u32[]{:S(2)}) collective-permute-start(bf16[304,128]{1,0:T(8,128)(2,1)} %get-tuple-element.115), channel_id=1, source_target_pairs={{0,2},{1,3},{2,0},{3,1},{4,6},{5,7},{6,4},{7,5},{8,10},{9,11},{10,... | collective-permute-start | bytes 233480 | tf_op jit(solution)/shard_map/ppermute | solution.py:107
  323.7 8.3 %collective-permute-start.30 = (bf16[304,128]{1,0:T(8,128)(2,1)}, bf16[304,128]{1,0:T(8,128)(2,1)S(1)}, u32[]{:S(2)}, u32[]{:S(2)}) collective-permute-start(bf16[304,128]{1,0:T(8,128)(2,1)} %get-tuple-element.116), channel_id=1, source_target_pairs={{0,4},{1,5},{2,6},{3,7},{4,0},{5,1},{6,2},{7,3},{8,12},{9,13},{10,... | collective-permute-start | bytes 233480 | tf_op jit(solution)/shard_map/ppermute | solution.py:107
  324.8 7.2 %collective-permute-start.31 = (bf16[304,128]{1,0:T(8,128)(2,1)}, bf16[304,128]{1,0:T(8,128)(2,1)S(1)}, u32[]{:S(2)}, u32[]{:S(2)}) collective-permute-start(bf16[304,128]{1,0:T(8,128)(2,1)} %get-tuple-element.117), channel_id=1, source_target_pairs={{0,6},{1,7},{2,4},{3,5},{4,2},{5,3},{6,0},{7,1},{8,14},{9,15},{10,... | collective-permute-start | bytes 233480 | tf_op jit(solution)/shard_map/ppermute | solution.py:107
  (35 other events, 185.6 us)
where the time goes:
time: 344 us; the launch traced here: 342 us
  waiting for transfers between devices  153 us (44%)
  Pallas kernels  115 us (33%)
  starting transfers between devices  55 us (16%)
  local copies, waits for them, and re-layouts  16 us (5%)
    ppermute x21, waiting for transfers between devices, row_swap(): lax.ppermute(x, 'row', swaps('row', k))  99.7 us
    all_to_all x6, waiting for transfers between devices, exchange(): return lax.all_to_all(pieces, ('row', 'col'), 0, 0, tiled=True)  45.7 us
    ppermute x21, starting transfers between devices, row_swap(): lax.ppermute(x, 'row', swaps('row', k))  24.5 us
    all_to_all x6, starting transfers between devices, exchange(): return lax.all_to_all(pieces, ('row', 'col'), 0, 0, tiled=True)  18.5 us
    pallas_call x1, Pallas kernels, expert_forward(): call(partial(expert_forward_kernel, rows, near), 'expert_forward', (shape...  18.4 us
    pallas_call x1, Pallas kernels, attention_backward(): call(partial(backward_kernel, n, far, parts), 'attention_backward', tuple...  15.7 us
    pallas_call x2, Pallas kernels, dispatch(): call(partial(dispatch_kernel, n), 'dispatch', shape((E * CAP, w), BF16),...  13.6 us
    pallas_call x1, Pallas kernels, expert_backward(): call(partial(expert_backward_kernel, rows, near), 'expert_backward', (sha...  12.4 us
  transfers between devices with their start and end apart: 38, of which 23 were waited for; matrix products, arithmetic and copies ran while one was open for 4% of the time, Pallas kernels for 32%

commit v1 on v0

--- a/solution.py
+++ b/solution.py
@@ -15,6 +15,7 @@
 CAP = 120
 EPS_NORM = 1e-06
 VMEM = 60 * 2**20
+SMALL = 24 * 2**20
 TILE = 480
 UNROLL = 4
 F32 = jnp.float32
@@ -222,7 +223,7 @@
     return x.reshape(t // ROWS, ROWS, w)[:, :SEQ].reshape(-1, w)
 
 
-def call(kernel, name, out_shape, n_in, scalars=0, scratch=(), flops=0, moved=0, **kw):
+def call(kernel, name, out_shape, n_in, scalars=0, scratch=(), flops=0, moved=0, limit=VMEM, **kw):
     smem = pl.BlockSpec(memory_space=pltpu.SMEM)
     vmem = pl.BlockSpec(memory_space=pltpu.VMEM)
     return pl.pallas_call(
@@ -232,7 +233,7 @@
         in_specs=[smem] * scalars + [vmem] * n_in,
         out_specs=jax.tree.map(lambda _: vmem, out_shape),
         scratch_shapes=list(scratch),
-        compiler_params=pltpu.CompilerParams(vmem_limit_bytes=VMEM),
+        compiler_params=pltpu.CompilerParams(vmem_limit_bytes=limit),
         cost_estimate=pl.CostEstimate(flops=flops, bytes_accessed=moved, transcendentals=0),
         **kw,
     )
@@ -321,7 +322,7 @@
 
 
 def slot_table(routes, keep):
-    return call(slots_kernel, "slots", shape(routes.shape, jnp.int32), 2)(routes, keep)
+    return call(slots_kernel, "slots", shape(routes.shape, jnp.int32), 2, limit=SMALL)(routes, keep)
 
 
 def dispatch_kernel(n, where_ref, slots_ref, *refs):
@@ -362,6 +363,7 @@
         scratch=[pltpu.VMEM((n * part, w), BF16)],
         flops=2 * E * CAP * n * part * w,
         moved=2 * (E * CAP + n * part) * w,
+        limit=SMALL,
     )(here, slots, *pieces)
 
 
@@ -395,6 +397,7 @@
         scalars=1,
         flops=2 * E * CAP * n * part * w,
         moved=2 * (E * CAP + n * part) * w,
+        limit=SMALL,
     )(here, columns, got)
 
 
@@ -424,6 +427,7 @@
         scalars=1,
         flops=2 * E * CAP * t * w,
         moved=2 * (E * CAP + 3 * t) * w,
+        limit=SMALL,
     )(here, columns, got, tokens, *pieces)
 
 
@@ -540,7 +544,7 @@
     ) = refs[3 * n : 3 * n + 8]
     sends = refs[3 * n + 8 : 4 * n + 8]
     refs = refs[4 * n + 8 :]
-    outs, (x_s, c_s, g_s, n1_s, ga_s, gp_s, tg_s, sums_s) = refs[:-8], refs[-8:]
+    outs, (x_s, c_s, g_s, n1_s, ga_s, gp_s, tg_s, sums_s, totals_s) = refs[:-9], refs[-9:]
     here = where_ref[0]
     w = pieces[0].shape[1]
     for k in range(n):
@@ -550,7 +554,7 @@
     width = n * w
     pairs = width // (2 * HD)
     low = lax.broadcasted_iota(jnp.int32, (1, 2 * HD), 1) < HD
-    lanes = lax.broadcasted_iota(jnp.int32, (1, 128), 1)
+    real = lax.broadcasted_iota(jnp.int32, (ROWS, 1), 0) < SEQ
     scale = HD ** (-0.5)
     sums_s[...] = jnp.zeros_like(sums_s)
 
@@ -566,28 +570,29 @@
         ga_s[rows, :] = grad_attn
         tg_s[rows, :] = dot(grad_attn, mix_ref[...], ((1,), (0,))).astype(BF16)
 
+        totals_s[...] = totals_ref[rows, :].T
+
         def head_pair(pair, carry):
             q_pair, k_pair, v_pair = (
                 project_ref[rows, block(j * pairs + pair, 2 * HD)] for j in range(3)
             )
             g_pair = tg_s[rows, block(pair, 2 * HD)]
-            totals = totals_ref[rows, :]
             got = []
             for head in range(2):
-                scores = head_scores(q_pair, k_pair, low, head)
-                total = jnp.sum(
-                    jnp.where(lanes == 2 * pair + head, totals, 0.0), axis=1, keepdims=True
-                )
-                probs = jnp.exp(scores - total)
-                g_head = jnp.where(low if head == 0 else ~low, g_pair, jnp.zeros_like(g_pair))
-                grad_probs = dot(g_head, v_pair, ((1,), (1,)))
-                row_dot = jnp.sum(probs * grad_probs, axis=1, keepdims=True)
-                grad_scores = (probs * (grad_probs - row_dot)).astype(BF16)
+                mine = low if head == 0 else ~low
+                q_head = jnp.where(mine, q_pair, jnp.zeros_like(q_pair))
+                g_head = jnp.where(mine, g_pair, jnp.zeros_like(g_pair))
+                scores = dot(k_pair, q_head, ((1,), (1,))) * scale
+                probs = jnp.exp(scores - totals_s[pl.ds(2 * pair + head, 1), :])
+                probs = jnp.where(real, probs, 0.0)
+                grad_probs = dot(v_pair, g_head, ((1,), (1,)))
+                dots = jnp.sum(probs * grad_probs, axis=0, keepdims=True)
+                grad_scores = (probs * (grad_probs - dots)).astype(BF16)
                 got.append(
                     (
-                        dot(grad_scores, k_pair, ((1,), (0,))) * scale,
-                        dot(grad_scores, q_pair, ((0,), (0,))) * scale,
-                        dot(probs.astype(BF16), g_pair, ((0,), (0,))),
+                        dot(grad_scores, k_pair, ((0,), (0,))) * scale,
+                        dot(grad_scores, q_pair, ((1,), (0,))) * scale,
+                        dot(probs.astype(BF16), g_pair, ((1,), (0,))),
                     )
                 )
             for j in range(3):
@@ -647,7 +652,7 @@
     width = n * w
     scratch = [pltpu.VMEM((t, width), F32)] * 3 + [pltpu.VMEM((t, width), BF16)] * 2
     scratch += [pltpu.VMEM((t, 3 * width), BF16), pltpu.VMEM((t, width), BF16)]
-    scratch += [pltpu.VMEM((8, width), F32)]
+    scratch += [pltpu.VMEM((8, width), F32), pltpu.VMEM((128, ROWS), F32)]
     if parts is None:
         outs = (
             shape((3 * width, width), F32),
@@ -727,6 +732,7 @@
         tuple(shape(own.shape[1:], BF16) for _ in range(own.shape[0])),
         2,
         moved=6 * own.size,
+        limit=SMALL,
     )(own, got)
 
 
@@ -744,6 +750,7 @@
         tuple(shape((depth, w), BF16) for _ in range(far)),
         len(pieces),
         moved=10 * far * depth * w,
+        limit=SMALL,
     )(*pieces)
 
 
@@ -764,6 +771,7 @@
         tuple(shape((part, w), F32) for part in (*parts, E + 8)),
         len(pieces),
         moved=12 * pieces[0].size,
+        limit=SMALL,
     )(*pieces)
 
 
@@ -1035,7 +1043,7 @@
     def to_experts(x, *earlier):
         return exchange(after(x.reshape(E, CAP, width_part), *earlier))
 
-    x_got = to_experts(dispatch(here, slots, normed), w_got)
+    x_got = to_experts(dispatch(here, slots, normed), w_got, columns)
     cot_got = to_experts(dispatch(nowhere, slots, [cot]), x_got, *others)
     moved, x_rows, act, slope, res, gates = expert_forward(
         expert, x_got, w_got, router_t, rows, near
@@ -1063,8 +1071,10 @@
 
     if tiled:
         own, other = outs
-        got = row_swap(add_core(own, core_swap(other)))
-        got = far_swap(add_rows(got))
+        mine = add_core(own, core_swap(other))
+        sends = [after(x, mine) for x in sends]
+        got = far_swap(add_rows(row_swap(mine)))
+        got[0] = after(got[0], expert_in_grad)
         qkv_grad, mix_grad, tail = add_far(got, parts)
     else:
         qkv_grad_t, mix_grad_t, tail = outs

time: 344 us -> 337 us (0.980)
  Pallas kernels: 115 us -> 103 us
  waiting for transfers between devices: 153 us -> 159 us
  local copies, waits for them, and re-layouts: 16 us -> 11 us
  starting transfers between devices: 55 us -> 58.7 us
    ppermute x21, waiting for transfers between devices: 99.7 us -> 109 us  [row_swap(): lax.ppermute(x, 'row', swaps('row', k))]
    ppermute x6, waiting for transfers between devices: 7.19 us -> 2.21 us  [far_swap(): lax.ppermute(x, 'col', swaps('col', 2 * k))]
  transfers between devices with their start and end apart: 38 -> 38, of which waited for: 23 -> 22; matrix products, arithmetic and copies ran while one was open for 4% -> 2% of each run, Pallas kernels for 32% -> 31%
where the time goes in v1:
time: 337 us; the launch traced here: 336 us
  waiting for transfers between devices  159 us (47%)
  Pallas kernels  103 us (31%)
  starting transfers between devices  58.7 us (17%)
  local copies, waits for them, and re-layouts  11 us (3%)
    ppermute x21, waiting for transfers between devices, row_swap(): lax.ppermute(x, 'row', swaps('row', k))  109 us
    all_to_all x6, waiting for transfers between devices, exchange(): return lax.all_to_all(pieces, ('row', 'col'), 0, 0, tiled=True)  45.2 us
    ppermute x21, starting transfers between devices, row_swap(): lax.ppermute(x, 'row', swaps('row', k))  24.2 us
    all_to_all x6, starting transfers between devices, exchange(): return lax.all_to_all(pieces, ('row', 'col'), 0, 0, tiled=True)  19.2 us
    pallas_call x1, Pallas kernels, expert_forward(): call(partial(expert_forward_kernel, rows, near), 'expert_forward', (shape...  18.4 us
    pallas_call x1, Pallas kernels, attention_backward(): call(partial(backward_kernel, n, far, parts), 'attention_backward', tuple...  15.3 us
    ppermute x6, starting transfers between devices, far_swap(): lax.ppermute(x, 'col', swaps('col', 2 * k))  14.6 us
    pallas_call x1, Pallas kernels, expert_backward(): call(partial(expert_backward_kernel, rows, near), 'expert_backward', (sha...  12.4 us
  transfers between devices with their start and end apart: 38, of which 22 were waited for; matrix products, arithmetic and copies ran while one was open for 2% of the time, Pallas kernels for 31%

profile of v1, /device:TPU:0, one launch (start us, length us, event | category | flops | bytes accessed | tf_op | source)
XLA Modules:
  0.0 335.9 jit_solution(1548782584560987116)
XLA Ops:
  1.5 3.0 collective-permute-start.3
  4.5 2.6 collective-permute-start.4
  7.1 3.8 %pack_weights.1 = bf16[32,128,512]{2,1,0:T(8,128)(2,1)} custom-call(bf16[32,128,256]{2,1,0:T(8,128)(2,1)} %in_ref.1, bf16[32,64,512]{2,1,0:T(8,128)(2,1)} %bitcast.63), custom_call_target="tpu_custom_call" | custom-call | bytes 8388608 | tf_op jit(solution)/shard_map/pack_weights/pallas_call | solution.py:273
  13.4 4.2 %all-to-all-start = ((bf16[32,128,512]{2,1,0:T(8,128)(2,1)}), bf16[32,128,512]{2,1,0:T(8,128)(2,1)}, u32[]{:S(2)}, u32[]{:S(2)}) async-start(bf16[32,128,512]{2,1,0:T(8,128)(2,1)} %pack_weights.1), calls=%async_computation | async-start | bytes 8388608 | tf_op jit(solution)/shard_map/all_to_all | solution.py:37
  17.5 1.8 collective-permute-start.6
  21.1 35.9 %collective-permute-done.6.refs_1_ = bf16[1072,128]{1,0:T(8,128)(2,1)S(1)} collective-permute-done((bf16[1072,128]{1,0:T(8,128)(2,1)S(1)}, bf16[1072,128]{1,0:T(8,128)(2,1)S(1)}, u32[]{:S(2)}, u32[]{:S(2)}) %collective-permute-start.6) | collective-permute-done | bytes 274464 | tf_op jit(solution)/shard_map/ppermute | solution.py:93
  57.8 8.3 %collective-permute-done.8.refs_3_ = bf16[1072,128]{1,0:T(8,128)(2,1)S(1)} collective-permute-done((bf16[1072,128]{1,0:T(8,128)(2,1)S(1)}, bf16[1072,128]{1,0:T(8,128)(2,1)S(1)}, u32[]{:S(2)}, u32[]{:S(2)}) %collective-permute-start.8) | collective-permute-done | bytes 274464 | tf_op jit(solution)/shard_map/ppermute | solution.py:93
  69.0 2.4 collective-permute-start.2
  72.0 3.3 gather_weights.1
  75.3 3.3 collective-permute-done.1.refs_2_.refs_6_
  79.3 8.5 %attention_forward.1 = (bf16[416,128]{1,0:T(8,128)(2,1)}, bf16[416,128]{1,0:T(8,128)(2,1)}, bf16[416,128]{1,0:T(8,128)(2,1)}, bf16[416,128]{1,0:T(8,128)(2,1)}, ...) custom-call(s32[3]{0:T(128)} %pad_add_fusion.where_ref, ...), custom_call_target="tpu_custom_call" | custom-call | flops 1308622848 | bytes 4194304 | tf_op jit(solution)/shard_map/attention_forward/pallas_call | solution.py:516
  87.8 3.9 %collective-permute-start.13 = (bf16[416,128]{1,0:T(8,128)(2,1)}, bf16[416,128]{1,0:T(8,128)(2,1)S(1)}, u32[]{:S(2)}, u32[]{:S(2)}) collective-permute-start(bf16[416,128]{1,0:T(8,128)(2,1)} %get-tuple-element.80), channel_id=1, source_target_pairs={{0,8},{8,0},{16,24},{24,16},{1,9},{9,1},{17,25},{25,17},{2,10},{10... | collective-permute-start | bytes 319496 | tf_op jit(solution)/shard_map/ppermute | solution.py:93
  94.3 2.4 collective-permute-done.13.refs_1_
  96.6 1.7 collective-permute-done.14.refs_2_
  100.1 6.3 %dispatch.2 = bf16[3840,128]{1,0:T(8,128)(2,1)} custom-call(s32[3]{0:T(128)S(1)} %copy-done.1, s32[2,1664]{1,0:T(2,128)S(1)} %slots.1.slots_ref, bf16[416,128]{1,0:T(8,128)(2,1)S(1)} %copy-done.8, bf16[416,128]{1,0:T(8,128)(2,1)S(1)} %collective-permute-done.13.refs_1_, bf16[416,128]{1,0:T(8,128)(2,1)S(1)} %collective-permute-done.14.refs_2_, ...), custom_call_target="tpu_custom_call" | custom-call | flops 1635778560 | bytes 1409024 | tf_op jit(solution)/shard_map/dispatch/pallas_call | solution.py:357
  106.3 6.3 %all-to-all-done.w_ref = bf16[32,128,512]{2,1,0:T(8,128)(2,1)} async-done(((bf16[32,128,512]{2,1,0:T(8,128)(2,1)}), bf16[32,128,512]{2,1,0:T(8,128)(2,1)}, u32[]{:S(2)}, u32[]{:S(2)}) %all-to-all-start) | async-done | bytes 4194336 | tf_op jit(solution)/shard_map/all_to_all | solution.py:37
  112.6 2.6 all-to-all-start.1
  115.2 1.7 collective-permute-start.16
  116.9 1.5 collective-permute-start.17
  118.8 5.7 %dispatch.3 = bf16[3840,128]{1,0:T(8,128)(2,1)} custom-call(s32[1]{0:T(128)} %constant.72.clone.1.where_ref, s32[2,1664]{1,0:T(2,128)S(1)} %slots.1.slots_ref, bf16[1664,128]{1,0:T(8,128)(2,1)S(1)} %bitcast.57), custom_call_target="tpu_custom_call" | custom-call | flops 1635778560 | bytes 1409024 | tf_op jit(solution)/shard_map/dispatch/pallas_call | solution.py:357
  124.5 6.3 %collective-permute-done.16.refs_1_.refs_9_ = bf16[2,416,128]{2,1,0:T(8,128)(2,1)S(1)} collective-permute-done((bf16[2,416,128]{2,1,0:T(8,128)(2,1)}, bf16[2,416,128]{2,1,0:T(8,128)(2,1)S(1)}, u32[]{:S(2)}, u32[]{:S(2)}) %collective-permute-start.16) | collective-permute-done | bytes 213024 | tf_op jit(solution)/shard_map/ppermute | solution.py:93
  131.6 6.7 %collective-permute-done.18.refs_3_.refs_11_ = bf16[2,416,128]{2,1,0:T(8,128)(2,1)S(1)} collective-permute-done((bf16[2,416,128]{2,1,0:T(8,128)(2,1)S(1)}, bf16[2,416,128]{2,1,0:T(8,128)(2,1)S(1)}, u32[]{:S(2)}, u32[]{:S(2)}) %collective-permute-start.18) | collective-permute-done | bytes 213024 | tf_op jit(solution)/shard_map/ppermute | solution.py:93
  138.9 2.5 all-to-all-done.1.got_ref
  141.4 3.4 all-to-all-start.2
  144.8 18.4 %expert_forward.1 = (bf16[32,120,128]{2,1,0:T(8,128)(2,1)}, bf16[960,512]{1,0:T(8,128)(2,1)}, bf16[4,960,512]{2,1,0:T(8,128)(2,1)}, bf16[4,960,512]{2,1,0:T(8,12...) custom-call(s32[1]{0:T(128)} %bitcast.6.e_ref, bf16[32,120,128]{2,1,0:T(8,128)(2,1)} %copy-done.11, ...), custom_call_target="tpu_custom_call" | custom-call | flops 4026531840 | bytes 16777216 | tf_op jit(solution)/shard_map/expert_forward/pallas_call | solution.py:868
  163.2 7.7 %all-to-all-done.2.got_ref = bf16[32,120,128]{2,1,0:T(8,128)(2,1)} async-done(((bf16[32,120,128]{2,1,0:T(8,128)(2,1)}), bf16[32,120,128]{2,1,0:T(8,128)(2,1)}, u32[]{:S(2)}, u32[]{:S(2)}) %all-to-all-start.2) | async-done | bytes 983072 | tf_op jit(solution)/shard_map/all_to_all | solution.py:37
  171.0 2.6 all-to-all-start.3
  173.6 12.4 %expert_backward.1 = (bf16[32,120,128]{2,1,0:T(8,128)(2,1)}, bf16[4,960,512]{2,1,0:T(8,128)(2,1)}, bf16[960,512]{1,0:T(8,128)(2,1)}, f32[32,512]{1,0:T(8,128)}) custom-call(s32[1]{0:T(128)} %bitcast.6.e_ref, bf16[32,120,128]{2,1,0:T(8,128)(2,1)} %all-to-all-done.2.got_ref, bf16[32,128,512]{2,1,0:T(8,128)(2,1)} %all-to-all-done.w_ref, ...), custom_call_target="tpu_custom_call" | custom-call | flops 4026531840 | bytes 16777216 | tf_op jit(solution)/shard_map/expert_backward/pallas_call | solution.py:917
  186.0 13.8 %all-to-all-done.3 = bf16[32,120,128]{2,1,0:T(8,128)(2,1)S(1)} async-done(((bf16[32,120,128]{2,1,0:T(8,128)(2,1)}), bf16[32,120,128]{2,1,0:T(8,128)(2,1)S(1)}, u32[]{:S(2)}, u32[]{:S(2)}) %all-to-all-start.3) | async-done | bytes 983072 | tf_op jit(solution)/shard_map/all_to_all | solution.py:37
  199.8 2.8 all-to-all-start.4
  202.6 11.1 %expert_grads.1 = bf16[32,128,512]{2,1,0:T(8,128)(2,1)} custom-call(bf16[960,512]{1,0:T(8,128)(2,1)} %get-tuple-element.93.x_ref, bf16[4,960,512]{2,1,0:T(8,128)(2,1)} %get-tuple-element.124.pre_ref, bf16[960,512]{1,0:T(8,128)(2,1)} %get-tuple-element.125.grad_res_ref, bf16[4,960,512]{2,1,0:T(8,128)(2,1)} %get-tuple-element.126.act_ref), custom_call_target="tpu_custom_call" | custom-call | flops 4026531840 | bytes 16777216 | tf_op jit(solution)/shard_map/expert_grads/pallas_call | solution.py:959
  213.7 14.9 %all-to-all-done.4 = bf16[32,120,128]{2,1,0:T(8,128)(2,1)S(1)} async-done(((bf16[32,120,128]{2,1,0:T(8,128)(2,1)}), bf16[32,120,128]{2,1,0:T(8,128)(2,1)S(1)}, u32[]{:S(2)}, u32[]{:S(2)}) %all-to-all-start.4) | async-done | bytes 983072 | tf_op jit(solution)/shard_map/all_to_all | solution.py:37
  228.6 3.6 %all-to-all-start.5 = ((bf16[32,128,512]{2,1,0:T(8,128)(2,1)}), bf16[32,128,512]{2,1,0:T(8,128)(2,1)}, u32[]{:S(2)}, u32[]{:S(2)}) async-start(bf16[32,128,512]{2,1,0:T(8,128)(2,1)} %expert_grads.1), calls=%async_computation.5 | async-start | bytes 8388608 | tf_op jit(solution)/shard_map/all_to_all | solution.py:37
  232.2 6.4 %combine.1 = (bf16[416,128]{1,0:T(8,128)(2,1)S(1)}, bf16[416,128]{1,0:T(8,128)(2,1)}, bf16[416,128]{1,0:T(8,128)(2,1)}, bf16[416,128]{1,0:T(8,128)(2,1)}) custom-call(s32[3]{0:T(128)S(1)} %copy-done.1, s32[1664,2]{1,0:T(8,128)S(1)} %bitcast.60, bf16[3840,128]{1,0:T(8,128)(2,1)S(1)} %bitcast.59), custom_call_target="tpu_custom_call" | custom-call | flops 1635778560 | bytes 1409024 | tf_op jit(solution)/shard_map/combine/pallas_call | solution.py:392
  238.6 1.6 collective-permute-start.19
  240.2 1.5 collective-permute-start.20
  242.1 5.8 %finish.1 = bf16[1664,128]{1,0:T(8,128)(2,1)S(1)} custom-call(s32[3]{0:T(128)S(1)} %copy-done.1, s32[1664,2]{1,0:T(8,128)S(1)} %bitcast.61, bf16[3840,128]{1,0:T(8,128)(2,1)S(1)} %bitcast.58, bf16[1664,128]{1,0:T(8,128)(2,1)S(1)} %bitcast.55, bf16[2,416,128]{2,1,0:T(8,128)(2,1)S(1)} %copy-done.7, ...), custom_call_target="tpu_custom_call" | custom-call | flops 1635778560 | bytes 2260992 | tf_op jit(solution)/shard_map/finish/pallas_call | solution.py:422
  248.8 14.4 %collective-permute-done.19.refs_1_ = bf16[416,128]{1,0:T(8,128)(2,1)S(1)} collective-permute-done((bf16[416,128]{1,0:T(8,128)(2,1)}, bf16[416,128]{1,0:T(8,128)(2,1)S(1)}, u32[]{:S(2)}, u32[]{:S(2)}) %collective-permute-start.19) | collective-permute-done | bytes 106528 | tf_op jit(solution)/shard_map/ppermute | solution.py:93
  263.2 7.1 %collective-permute-done.21.refs_3_ = bf16[416,128]{1,0:T(8,128)(2,1)S(1)} collective-permute-done((bf16[416,128]{1,0:T(8,128)(2,1)}, bf16[416,128]{1,0:T(8,128)(2,1)S(1)}, u32[]{:S(2)}, u32[]{:S(2)}) %collective-permute-start.21) | collective-permute-done | bytes 106528 | tf_op jit(solution)/shard_map/ppermute | solution.py:93
  270.9 15.3 %attention_backward.1 = (bf16[416,128]{1,0:T(8,128)(2,1)}, bf16[416,128]{1,0:T(8,128)(2,1)}, bf16[416,128]{1,0:T(8,128)(2,1)}, bf16[416,128]{1,0:T(8,128)(2,1)},...) custom-call(s32[3]{0:T(128)} %pad_add_fusion.where_ref, bf16[416,128]{1,0:T(8,128)(2,1)} %copy-done.9, ...), custom_call_target="tpu_custom_call" | custom-call | flops 3271557120 | bytes 8388608 | tf_op jit(solution)/shard_map/attention_backward/pallas_call | solution.py:669
  286.3 3.1 collective-permute-done.22.got_ref
  291.8 2.8 collective-permute-start.25
  295.2 3.0 collective-permute-done.23
  301.1 8.1 %collective-permute-done.26.refs_1_ = bf16[4,304,128]{2,1,0:T(8,128)(2,1)S(1)} collective-permute-done((bf16[4,304,128]{2,1,0:T(8,128)(2,1)S(1)}, bf16[4,304,128]{2,1,0:T(8,128)(2,1)S(1)}, u32[]{:S(2)}, u32[]{:S(2)}) %collective-permute-start.26) | collective-permute-done | bytes 311328 | tf_op jit(solution)/shard_map/ppermute | solution.py:93
  309.2 9.4 %collective-permute-done.28.refs_3_ = bf16[4,304,128]{2,1,0:T(8,128)(2,1)S(1)} collective-permute-done((bf16[4,304,128]{2,1,0:T(8,128)(2,1)S(1)}, bf16[4,304,128]{2,1,0:T(8,128)(2,1)S(1)}, u32[]{:S(2)}, u32[]{:S(2)}) %collective-permute-start.28) | collective-permute-done | bytes 311328 | tf_op jit(solution)/shard_map/ppermute | solution.py:93
  318.8 6.6 %collective-permute-start.29 = (bf16[304,128]{1,0:T(8,128)(2,1)S(1)}, bf16[304,128]{1,0:T(8,128)(2,1)S(1)}, u32[]{:S(2)}, u32[]{:S(2)}) collective-permute-start(bf16[304,128]{1,0:T(8,128)(2,1)S(1)} %get-tuple-element.130), channel_id=1, source_target_pairs={{0,2},{1,3},{2,0},{3,1},{4,6},{5,7},{6,4},{7,5},{8,10},{9,11},{10,... | collective-permute-start | bytes 233480 | tf_op jit(solution)/shard_map/ppermute | solution.py:108
  326.0 1.8 collective-permute-start.31
  328.8 5.1 %unpack_grads.1 = (f32[32,128,256]{2,1,0:T(8,128)}, f32[32,64,512]{2,1,0:T(8,128)}) custom-call(bf16[32,128,512]{2,1,0:T(8,128)(2,1)} %all-to-all-done.5.got_ref), custom_call_target="tpu_custom_call" | custom-call | bytes 12582912 | tf_op jit(solution)/shard_map/unpack_grads/pallas_call | solution.py:290
  (141 shorter events, 27.6 us)
Async XLA Ops:
  1.5 9.5 %collective-permute-start.3 = (bf16[256,128]{1,0:T(8,128)(2,1)S(1)}, bf16[256,128]{1,0:T(8,128)(2,1)S(1)}, u32[]{:S(2)}, u32[]{:S(2)}) collective-permute-start(bf16[256,128]{1,0:T(8,128)(2,1)S(1)} %pad_maximum_fusion.1), channel_id=1, source_target_pairs={{0,2},{1,3},{2,0},{3,1},{4,6},{5,7},{6,4},{7,5},{8,10},{9,11},{10,... | collective-permute-start | bytes 196616 | tf_op jit(solution)/shard_map/ppermute | solution.py:108
  4.5 7.3 %collective-permute-start.4 = (bf16[256,128]{1,0:T(8,128)(2,1)S(1)}, bf16[256,128]{1,0:T(8,128)(2,1)S(1)}, u32[]{:S(2)}, u32[]{:S(2)}) collective-permute-start(bf16[256,128]{1,0:T(8,128)(2,1)S(1)} %pad_maximum_fusion.1), channel_id=1, source_target_pairs={{0,4},{1,5},{2,6},{3,7},{4,0},{5,1},{6,2},{7,3},{8,12},{9,13},{10,... | collective-permute-start | bytes 196616 | tf_op jit(solution)/shard_map/ppermute | solution.py:108
  7.1 6.1 %collective-permute-start.5 = (bf16[256,128]{1,0:T(8,128)(2,1)S(1)}, bf16[256,128]{1,0:T(8,128)(2,1)S(1)}, u32[]{:S(2)}, u32[]{:S(2)}) collective-permute-start(bf16[256,128]{1,0:T(8,128)(2,1)S(1)} %pad_maximum_fusion.1), channel_id=1, source_target_pairs={{0,6},{1,7},{2,4},{3,5},{4,2},{5,3},{6,0},{7,1},{8,14},{9,15},{10,... | collective-permute-start | bytes 196616 | tf_op jit(solution)/shard_map/ppermute | solution.py:108
  13.3 43.7 %copy-start.12 = (bf16[1576,128]{1,0:T(8,128)(2,1)S(1)}, bf16[1576,128]{1,0:T(8,128)(2,1)}, u32[]{:S(2)}) copy-start(bf16[1576,128]{1,0:T(8,128)(2,1)} %param.13) | copy-start | bytes 1210372
  13.3 54.0 %copy-start.13 = (bf16[1576,128]{1,0:T(8,128)(2,1)S(1)}, bf16[1576,128]{1,0:T(8,128)(2,1)}, u32[]{:S(2)}) copy-start(bf16[1576,128]{1,0:T(8,128)(2,1)} %param.25) | copy-start | bytes 1210372
  13.4 99.2 %all-to-all-start = ((bf16[32,128,512]{2,1,0:T(8,128)(2,1)}), bf16[32,128,512]{2,1,0:T(8,128)(2,1)}, u32[]{:S(2)}, u32[]{:S(2)}) async-start(bf16[32,128,512]{2,1,0:T(8,128)(2,1)} %pack_weights.1), calls=%async_computation | async-start | bytes 8388608 | tf_op jit(solution)/shard_map/all_to_all | solution.py:37
  17.5 39.5 %collective-permute-start.6 = (bf16[1072,128]{1,0:T(8,128)(2,1)S(1)}, bf16[1072,128]{1,0:T(8,128)(2,1)S(1)}, u32[]{:S(2)}, u32[]{:S(2)}) collective-permute-start(bf16[1072,128]{1,0:T(8,128)(2,1)S(1)} %concatenate.11.refs_0_), channel_id=1, source_target_pairs={{0,8},{8,0},{16,24},{24,16},{1,9},{9,1},{17,25},{25,17},{2,10},{10... | collective-permute-start | bytes 823304 | tf_op jit(solution)/shard_map/ppermute | solution.py:93
  19.3 37.9 %collective-permute-start.7 = (bf16[1072,128]{1,0:T(8,128)(2,1)S(1)}, bf16[1072,128]{1,0:T(8,128)(2,1)S(1)}, u32[]{:S(2)}, u32[]{:S(2)}) collective-permute-start(bf16[1072,128]{1,0:T(8,128)(2,1)S(1)} %concatenate.11.refs_0_), channel_id=1, source_target_pairs={{0,16},{8,24},{16,0},{24,8},{1,17},{9,25},{17,1},{25,9},{2,18},{10... | collective-permute-start | bytes 823304 | tf_op jit(solution)/shard_map/ppermute | solution.py:93
  20.8 45.3 %collective-permute-start.8 = (bf16[1072,128]{1,0:T(8,128)(2,1)S(1)}, bf16[1072,128]{1,0:T(8,128)(2,1)S(1)}, u32[]{:S(2)}, u32[]{:S(2)}) collective-permute-start(bf16[1072,128]{1,0:T(8,128)(2,1)S(1)} %concatenate.11.refs_0_), channel_id=1, source_target_pairs={{0,24},{8,16},{16,8},{24,0},{1,25},{9,17},{17,9},{25,1},{2,26},{10... | collective-permute-start | bytes 823304 | tf_op jit(solution)/shard_map/ppermute | solution.py:93
  21.1 47.2 %collective-permute-start.9 = (bf16[1072,128]{1,0:T(8,128)(2,1)S(1)}, bf16[1072,128]{1,0:T(8,128)(2,1)S(1)}, u32[]{:S(2)}, u32[]{:S(2)}) collective-permute-start(bf16[1072,128]{1,0:T(8,128)(2,1)S(1)} %concatenate.11.refs_0_), channel_id=1, source_target_pairs={{0,1},{1,0},{2,3},{3,2},{4,5},{5,4},{6,7},{7,6},{8,9},{9,8},{10,11... | collective-permute-start | bytes 823304 | tf_op jit(solution)/shard_map/ppermute | solution.py:113
  57.0 15.0 %copy-start.14 = (bf16[1072,128]{1,0:T(8,128)(2,1)}, bf16[1072,128]{1,0:T(8,128)(2,1)S(1)}, u32[]{:S(2)}) copy-start(bf16[1072,128]{1,0:T(8,128)(2,1)S(1)} %collective-permute-done.6.refs_1_) | copy-start | bytes 823300
  57.0 12.0 %collective-permute-start.10 = (bf16[1072,128]{1,0:T(8,128)(2,1)S(1)}, bf16[1072,128]{1,0:T(8,128)(2,1)S(1)}, u32[]{:S(2)}, u32[]{:S(2)}) collective-permute-start(bf16[1072,128]{1,0:T(8,128)(2,1)S(1)} %collective-permute-done.6.refs_1_), channel_id=1, source_target_pairs={{0,1},{1,0},{2,3},{3,2},{4,5},{5,4},{6,7},{7,6},{8,9},{9,8},{10,11... | collective-permute-start | bytes 823304 | tf_op jit(solution)/shard_map/ppermute | solution.py:113
  57.2 14.8 %copy-start.15 = (bf16[1072,128]{1,0:T(8,128)(2,1)}, bf16[1072,128]{1,0:T(8,128)(2,1)S(1)}, u32[]{:S(2)}) copy-start(bf16[1072,128]{1,0:T(8,128)(2,1)S(1)} %collective-permute-done.7.refs_2_) | copy-start | bytes 823300
  57.2 14.7 %collective-permute-start.11 = (bf16[1072,128]{1,0:T(8,128)(2,1)S(1)}, bf16[1072,128]{1,0:T(8,128)(2,1)}, u32[]{:S(2)}, u32[]{:S(2)}) collective-permute-start(bf16[1072,128]{1,0:T(8,128)(2,1)S(1)} %collective-permute-done.7.refs_2_), channel_id=1, source_target_pairs={{0,1},{1,0},{2,3},{3,2},{4,5},{5,4},{6,7},{7,6},{8,9},{9,8},{10,11... | collective-permute-start | bytes 823304 | tf_op jit(solution)/shard_map/ppermute | solution.py:113
  66.1 5.9 %collective-permute-start.12 = (bf16[1072,128]{1,0:T(8,128)(2,1)S(1)}, bf16[1072,128]{1,0:T(8,128)(2,1)}, u32[]{:S(2)}, u32[]{:S(2)}) collective-permute-start(bf16[1072,128]{1,0:T(8,128)(2,1)S(1)} %collective-permute-done.8.refs_3_), channel_id=1, source_target_pairs={{0,1},{1,0},{2,3},{3,2},{4,5},{5,4},{6,7},{7,6},{8,9},{9,8},{10,11... | collective-permute-start | bytes 823304 | tf_op jit(solution)/shard_map/ppermute | solution.py:113
  66.9 8.5 %collective-permute-start = (bf16[416,128]{1,0:T(8,128)(2,1)}, bf16[416,128]{1,0:T(8,128)(2,1)}, u32[]{:S(2)}, u32[]{:S(2)}) collective-permute-start(bf16[416,128]{1,0:T(8,128)(2,1)} %get-tuple-element.169), channel_id=1, source_target_pairs={{0,8},{8,0},{16,24},{24,16},{1,9},{9,1},{17,25},{25,17},{2,10},{10... | collective-permute-start | bytes 319496 | tf_op jit(solution)/shard_map/ppermute | solution.py:93
  67.5 25.8 %copy-start.21 = (s32[1576,2]{0,1:T(2,128)S(1)}, s32[1576,2]{0,1:T(2,128)}, u32[]{:S(2)}) copy-start(s32[1576,2]{0,1:T(2,128)} %param.23) | copy-start | bytes 37828
  67.5 26.0 %copy-start.22 = (s32[1576,2]{0,1:T(2,128)S(1)}, s32[1576,2]{0,1:T(2,128)}, u32[]{:S(2)}) copy-start(s32[1576,2]{0,1:T(2,128)} %param.24) | copy-start | bytes 37828
  68.3 10.3 %collective-permute-start.1 = (bf16[416,128]{1,0:T(8,128)(2,1)}, bf16[416,128]{1,0:T(8,128)(2,1)S(1)}, u32[]{:S(2)}, u32[]{:S(2)}) collective-permute-start(bf16[416,128]{1,0:T(8,128)(2,1)} %get-tuple-element.168), channel_id=1, source_target_pairs={{0,16},{8,24},{16,0},{24,8},{1,17},{9,25},{17,1},{25,9},{2,18},{10... | collective-permute-start | bytes 319496 | tf_op jit(solution)/shard_map/ppermute | solution.py:93
  69.0 9.6 %collective-permute-start.2 = (bf16[416,128]{1,0:T(8,128)(2,1)S(1)}, bf16[416,128]{1,0:T(8,128)(2,1)S(1)}, u32[]{:S(2)}, u32[]{:S(2)}) collective-permute-start(bf16[416,128]{1,0:T(8,128)(2,1)S(1)} %get-tuple-element.167), channel_id=1, source_target_pairs={{0,24},{8,16},{16,8},{24,0},{1,25},{9,17},{17,9},{25,1},{2,26},{10... | collective-permute-start | bytes 319496 | tf_op jit(solution)/shard_map/ppermute | solution.py:93
  72.0 27.2 %copy-start.1 = (s32[3]{0:T(128)S(1)}, s32[3]{0:T(128)}, u32[]{:S(2)}) copy-start(s32[3]{0:T(128)} %pad_add_fusion.where_ref) | copy-start | bytes 40
  87.8 8.8 %collective-permute-start.13 = (bf16[416,128]{1,0:T(8,128)(2,1)}, bf16[416,128]{1,0:T(8,128)(2,1)S(1)}, u32[]{:S(2)}, u32[]{:S(2)}) collective-permute-start(bf16[416,128]{1,0:T(8,128)(2,1)} %get-tuple-element.80), channel_id=1, source_target_pairs={{0,8},{8,0},{16,24},{24,16},{1,9},{9,1},{17,25},{25,17},{2,10},{10... | collective-permute-start | bytes 319496 | tf_op jit(solution)/shard_map/ppermute | solution.py:93
  91.7 6.6 %collective-permute-start.14 = (bf16[416,128]{1,0:T(8,128)(2,1)}, bf16[416,128]{1,0:T(8,128)(2,1)S(1)}, u32[]{:S(2)}, u32[]{:S(2)}) collective-permute-start(bf16[416,128]{1,0:T(8,128)(2,1)} %get-tuple-element.81), channel_id=1, source_target_pairs={{0,16},{8,24},{16,0},{24,8},{1,17},{9,25},{17,1},{25,9},{2,18},{10... | collective-permute-start | bytes 319496 | tf_op jit(solution)/shard_map/ppermute | solution.py:93
  92.3 6.9 %collective-permute-start.15 = (bf16[416,128]{1,0:T(8,128)(2,1)}, bf16[416,128]{1,0:T(8,128)(2,1)S(1)}, u32[]{:S(2)}, u32[]{:S(2)}) collective-permute-start(bf16[416,128]{1,0:T(8,128)(2,1)} %get-tuple-element.82), channel_id=1, source_target_pairs={{0,24},{8,16},{16,8},{24,0},{1,25},{9,17},{17,9},{25,1},{2,26},{10... | collective-permute-start | bytes 319496 | tf_op jit(solution)/shard_map/ppermute | solution.py:93
  100.1 16.9 %copy-start.29 = (bf16[2,416,128]{2,1,0:T(8,128)(2,1)S(1)}, bf16[2,416,128]{2,1,0:T(8,128)(2,1)}, u32[]{:S(2)}) copy-start(bf16[2,416,128]{2,1,0:T(8,128)(2,1)} %get-tuple-element.89) | copy-start | bytes 638980
  100.1 18.4 %copy-start.28 = (bf16[2,416,128]{2,1,0:T(8,128)(2,1)S(1)}, bf16[2,416,128]{2,1,0:T(8,128)(2,1)}, u32[]{:S(2)}) copy-start(bf16[2,416,128]{2,1,0:T(8,128)(2,1)} %get-tuple-element.90) | copy-start | bytes 638980
  112.6 28.8 %all-to-all-start.1 = ((bf16[32,120,128]{2,1,0:T(8,128)(2,1)}), bf16[32,120,128]{2,1,0:T(8,128)(2,1)S(1)}, u32[]{:S(2)}, u32[]{:S(2)}) async-start(bf16[32,120,128]{2,1,0:T(8,128)(2,1)} %bitcast.24), calls=%async_computation.1 | async-start | bytes 1966080 | tf_op jit(solution)/shard_map/all_to_all | solution.py:37
  115.2 15.6 %collective-permute-start.16 = (bf16[2,416,128]{2,1,0:T(8,128)(2,1)}, bf16[2,416,128]{2,1,0:T(8,128)(2,1)S(1)}, u32[]{:S(2)}, u32[]{:S(2)}) collective-permute-start(bf16[2,416,128]{2,1,0:T(8,128)(2,1)} %get-tuple-element.88), channel_id=1, source_target_pairs={{0,8},{8,0},{16,24},{24,16},{1,9},{9,1},{17,25},{25,17},{2,10},{10... | collective-permute-start | bytes 638984 | tf_op jit(solution)/shard_map/ppermute | solution.py:93
  116.9 13.9 %collective-permute-start.17 = (bf16[2,416,128]{2,1,0:T(8,128)(2,1)S(1)}, bf16[2,416,128]{2,1,0:T(8,128)(2,1)S(1)}, u32[]{:S(2)}, u32[]{:S(2)}) collective-permute-start(bf16[2,416,128]{2,1,0:T(8,128)(2,1)S(1)} %copy-done.29), channel_id=1, source_target_pairs={{0,16},{8,24},{16,0},{24,8},{1,17},{9,25},{17,1},{25,9},{2,18},{10... | collective-permute-start | bytes 638984 | tf_op jit(solution)/shard_map/ppermute | solution.py:93
  118.4 19.8 %collective-permute-start.18 = (bf16[2,416,128]{2,1,0:T(8,128)(2,1)S(1)}, bf16[2,416,128]{2,1,0:T(8,128)(2,1)S(1)}, u32[]{:S(2)}, u32[]{:S(2)}) collective-permute-start(bf16[2,416,128]{2,1,0:T(8,128)(2,1)S(1)} %copy-done.28), channel_id=1, source_target_pairs={{0,24},{8,16},{16,8},{24,0},{1,25},{9,17},{17,9},{25,1},{2,26},{10... | collective-permute-start | bytes 638984 | tf_op jit(solution)/shard_map/ppermute | solution.py:93
  130.9 111.2 %copy-start.2 = (bf16[2,416,128]{2,1,0:T(8,128)(2,1)}, bf16[2,416,128]{2,1,0:T(8,128)(2,1)S(1)}, u32[]{:S(2)}) copy-start(bf16[2,416,128]{2,1,0:T(8,128)(2,1)S(1)} %collective-permute-done.16.refs_1_.refs_9_) | copy-start | bytes 638980
  141.4 29.5 %all-to-all-start.2 = ((bf16[32,120,128]{2,1,0:T(8,128)(2,1)}), bf16[32,120,128]{2,1,0:T(8,128)(2,1)}, u32[]{:S(2)}, u32[]{:S(2)}) async-start(bf16[32,120,128]{2,1,0:T(8,128)(2,1)} %bitcast.27), calls=%async_computation.2 | async-start | bytes 1966080 | tf_op jit(solution)/shard_map/all_to_all | solution.py:37
  171.0 28.8 %all-to-all-start.3 = ((bf16[32,120,128]{2,1,0:T(8,128)(2,1)}), bf16[32,120,128]{2,1,0:T(8,128)(2,1)S(1)}, u32[]{:S(2)}, u32[]{:S(2)}) async-start(bf16[32,120,128]{2,1,0:T(8,128)(2,1)} %get-tuple-element.92), calls=%async_computation.3 | async-start | bytes 1966080 | tf_op jit(solution)/shard_map/all_to_all | solution.py:37
  199.8 28.8 %all-to-all-start.4 = ((bf16[32,120,128]{2,1,0:T(8,128)(2,1)}), bf16[32,120,128]{2,1,0:T(8,128)(2,1)S(1)}, u32[]{:S(2)}, u32[]{:S(2)}) async-start(bf16[32,120,128]{2,1,0:T(8,128)(2,1)} %get-tuple-element.98), calls=%async_computation.4 | async-start | bytes 1966080 | tf_op jit(solution)/shard_map/all_to_all | solution.py:37
  228.6 100.2 %all-to-all-start.5 = ((bf16[32,128,512]{2,1,0:T(8,128)(2,1)}), bf16[32,128,512]{2,1,0:T(8,128)(2,1)}, u32[]{:S(2)}, u32[]{:S(2)}) async-start(bf16[32,128,512]{2,1,0:T(8,128)(2,1)} %expert_grads.1), calls=%async_computation.5 | async-start | bytes 8388608 | tf_op jit(solution)/shard_map/all_to_all | solution.py:37
  238.6 24.6 %collective-permute-start.19 = (bf16[416,128]{1,0:T(8,128)(2,1)}, bf16[416,128]{1,0:T(8,128)(2,1)S(1)}, u32[]{:S(2)}, u32[]{:S(2)}) collective-permute-start(bf16[416,128]{1,0:T(8,128)(2,1)} %get-tuple-element.101), channel_id=1, source_target_pairs={{0,8},{8,0},{16,24},{24,16},{1,9},{9,1},{17,25},{25,17},{2,10},{10... | collective-permute-start | bytes 319496 | tf_op jit(solution)/shard_map/ppermute | solution.py:93
  240.2 23.0 %collective-permute-start.20 = (bf16[416,128]{1,0:T(8,128)(2,1)}, bf16[416,128]{1,0:T(8,128)(2,1)S(1)}, u32[]{:S(2)}, u32[]{:S(2)}) collective-permute-start(bf16[416,128]{1,0:T(8,128)(2,1)} %get-tuple-element.102), channel_id=1, source_target_pairs={{0,16},{8,24},{16,0},{24,8},{1,17},{9,25},{17,1},{25,9},{2,18},{10... | collective-permute-start | bytes 319496 | tf_op jit(solution)/shard_map/ppermute | solution.py:93
  241.7 28.6 %collective-permute-start.21 = (bf16[416,128]{1,0:T(8,128)(2,1)}, bf16[416,128]{1,0:T(8,128)(2,1)S(1)}, u32[]{:S(2)}, u32[]{:S(2)}) collective-permute-start(bf16[416,128]{1,0:T(8,128)(2,1)} %get-tuple-element.103), channel_id=1, source_target_pairs={{0,24},{8,16},{16,8},{24,0},{1,25},{9,17},{17,9},{25,1},{2,26},{10... | collective-permute-start | bytes 319496 | tf_op jit(solution)/shard_map/ppermute | solution.py:93
  286.2 3.2 collective-permute-start.22
  291.0 7.3 %collective-permute-start.23 = (bf16[416,128]{1,0:T(8,128)(2,1)}, bf16[416,128]{1,0:T(8,128)(2,1)S(1)}, u32[]{:S(2)}, u32[]{:S(2)}) collective-permute-start(bf16[416,128]{1,0:T(8,128)(2,1)} %get-tuple-element.116), channel_id=1, source_target_pairs={{0,24},{8,16},{16,8},{24,0},{1,25},{9,17},{17,9},{25,1},{2,26},{10... | collective-permute-start | bytes 319496 | tf_op jit(solution)/shard_map/ppermute | solution.py:93
  291.1 9.0 %collective-permute-start.24 = (bf16[416,128]{1,0:T(8,128)(2,1)}, bf16[416,128]{1,0:T(8,128)(2,1)S(1)}, u32[]{:S(2)}, u32[]{:S(2)}) collective-permute-start(bf16[416,128]{1,0:T(8,128)(2,1)} %get-tuple-element.118), channel_id=1, source_target_pairs={{0,16},{8,24},{16,0},{24,8},{1,17},{9,25},{17,1},{25,9},{2,18},{10... | collective-permute-start | bytes 319496 | tf_op jit(solution)/shard_map/ppermute | solution.py:93
  291.8 8.3 %collective-permute-start.25 = (bf16[416,128]{1,0:T(8,128)(2,1)}, bf16[416,128]{1,0:T(8,128)(2,1)S(1)}, u32[]{:S(2)}, u32[]{:S(2)}) collective-permute-start(bf16[416,128]{1,0:T(8,128)(2,1)} %get-tuple-element.120), channel_id=1, source_target_pairs={{0,8},{8,0},{16,24},{24,16},{1,9},{9,1},{17,25},{25,17},{2,10},{10... | collective-permute-start | bytes 319496 | tf_op jit(solution)/shard_map/ppermute | solution.py:93
  294.6 14.6 %collective-permute-start.26 = (bf16[4,304,128]{2,1,0:T(8,128)(2,1)S(1)}, bf16[4,304,128]{2,1,0:T(8,128)(2,1)S(1)}, u32[]{:S(2)}, u32[]{:S(2)}) collective-permute-start(bf16[4,304,128]{2,1,0:T(8,128)(2,1)S(1)} %get-tuple-element.113), channel_id=1, source_target_pairs={{0,8},{8,0},{16,24},{24,16},{1,9},{9,1},{17,25},{25,17},{2,10},{10... | collective-permute-start | bytes 933896 | tf_op jit(solution)/shard_map/ppermute | solution.py:93
  294.6 14.6 %collective-permute-start.27 = (bf16[4,304,128]{2,1,0:T(8,128)(2,1)S(1)}, bf16[4,304,128]{2,1,0:T(8,128)(2,1)S(1)}, u32[]{:S(2)}, u32[]{:S(2)}) collective-permute-start(bf16[4,304,128]{2,1,0:T(8,128)(2,1)S(1)} %get-tuple-element.114), channel_id=1, source_target_pairs={{0,16},{8,24},{16,0},{24,8},{1,17},{9,25},{17,1},{25,9},{2,18},{10... | collective-permute-start | bytes 933896 | tf_op jit(solution)/shard_map/ppermute | solution.py:93
  298.3 20.3 %collective-permute-start.28 = (bf16[4,304,128]{2,1,0:T(8,128)(2,1)S(1)}, bf16[4,304,128]{2,1,0:T(8,128)(2,1)S(1)}, u32[]{:S(2)}, u32[]{:S(2)}) collective-permute-start(bf16[4,304,128]{2,1,0:T(8,128)(2,1)S(1)} %get-tuple-element.115), channel_id=1, source_target_pairs={{0,24},{8,16},{16,8},{24,0},{1,25},{9,17},{17,9},{25,1},{2,26},{10... | collective-permute-start | bytes 933896 | tf_op jit(solution)/shard_map/ppermute | solution.py:93
  318.8 15.1 %collective-permute-start.29 = (bf16[304,128]{1,0:T(8,128)(2,1)S(1)}, bf16[304,128]{1,0:T(8,128)(2,1)S(1)}, u32[]{:S(2)}, u32[]{:S(2)}) collective-permute-start(bf16[304,128]{1,0:T(8,128)(2,1)S(1)} %get-tuple-element.130), channel_id=1, source_target_pairs={{0,2},{1,3},{2,0},{3,1},{4,6},{5,7},{6,4},{7,5},{8,10},{9,11},{10,... | collective-permute-start | bytes 233480 | tf_op jit(solution)/shard_map/ppermute | solution.py:108
  325.3 8.6 %collective-permute-start.30 = (bf16[304,128]{1,0:T(8,128)(2,1)S(1)}, bf16[304,128]{1,0:T(8,128)(2,1)S(1)}, u32[]{:S(2)}, u32[]{:S(2)}) collective-permute-start(bf16[304,128]{1,0:T(8,128)(2,1)S(1)} %get-tuple-element.131), channel_id=1, source_target_pairs={{0,4},{1,5},{2,6},{3,7},{4,0},{5,1},{6,2},{7,3},{8,12},{9,13},{10,... | collective-permute-start | bytes 233480 | tf_op jit(solution)/shard_map/ppermute | solution.py:108
  326.0 7.9 %collective-permute-start.31 = (bf16[304,128]{1,0:T(8,128)(2,1)S(1)}, bf16[304,128]{1,0:T(8,128)(2,1)S(1)}, u32[]{:S(2)}, u32[]{:S(2)}) collective-permute-start(bf16[304,128]{1,0:T(8,128)(2,1)S(1)} %get-tuple-element.132), channel_id=1, source_target_pairs={{0,6},{1,7},{2,4},{3,5},{4,2},{5,3},{6,0},{7,1},{8,14},{9,15},{10,... | collective-permute-start | bytes 233480 | tf_op jit(solution)/shard_map/ppermute | solution.py:108
  (25 other events, 116.0 us)

commit v2 on v1

--- a/solution.py
+++ b/solution.py
@@ -754,25 +754,34 @@
     )(*pieces)
 
 
-def add_far_kernel(n, parts, *refs):
-    pieces, (qkv_ref, mix_ref, small_ref) = refs[:n], refs[n:]
+def add_far_kernel(n, parts, thin, where_ref, *refs):
+    pieces, (qkv_ref, mix_ref, router_ref, *norm_refs) = refs[:n], refs[n:]
     total = sum(piece[...].astype(F32) for piece in pieces)
     first, second = parts
     qkv_ref[...] = total[:first]
     mix_ref[...] = total[first : first + second]
-    small_ref[...] = total[first + second : first + second + E + 8]
-
-
-def add_far(pieces, parts):
+    tail = total[first + second : first + second + E + 8]
+    w = tail.shape[1]
+    col = 2 * where_ref[1] + where_ref[2]
+    tail = pltpu.roll(tail, lax.rem(w - col * thin, w), 1)
+    router_ref[...] = tail[:E].T[:thin]
+    for j, norm_ref in enumerate(norm_refs):
+        norm_ref[...] = tail[E + j : E + j + 1, :thin]
+
+
+def add_far(where, pieces, parts, thin):
     w = pieces[0].shape[1]
     return call(
-        partial(add_far_kernel, len(pieces), parts),
+        partial(add_far_kernel, len(pieces), parts, thin),
         "add_far",
-        tuple(shape((part, w), F32) for part in (*parts, E + 8)),
+        tuple(shape((part, w), F32) for part in parts)
+        + (shape((thin, E), F32),)
+        + tuple(shape((1, thin), F32) for _ in range(4)),
         len(pieces),
+        scalars=1,
         moved=12 * pieces[0].size,
         limit=SMALL,
-    )(*pieces)
+    )(where, *pieces)
 
 
 def hidden_block(w_ref, i, rows, near):
@@ -1075,7 +1084,10 @@
         sends = [after(x, mine) for x in sends]
         got = far_swap(add_rows(row_swap(mine)))
         got[0] = after(got[0], expert_in_grad)
-        qkv_grad, mix_grad, tail = add_far(got, parts)
+        qkv_grad, mix_grad, router_grad, *norm_grads = add_far(
+            here, got, parts, width_part // cols
+        )
+        norm_grads = [x.reshape(-1) for x in norm_grads]
     else:
         qkv_grad_t, mix_grad_t, tail = outs
         shares = jnp.concatenate(
@@ -1088,20 +1100,22 @@
         )
         sums = reduce_all(shares)
         qkv_grad, mix_grad, tail = jnp.split(sums, [qkv_part, qkv_part + mix_part])
-    thin = width_part // cols
-    tail = lax.dynamic_slice_in_dim(tail, col * thin, thin, axis=1)
+        thin = width_part // cols
+        tail = lax.dynamic_slice_in_dim(tail, col * thin, thin, axis=1)
+        router_grad = tail[:E].T
+        norm_grads = [tail[E + j] for j in range(4)]
     tokens_grad = jnp.concatenate(in_order(row_swap(sends), row), axis=0)
     tokens_grad = cut_images(tokens_grad).astype(F32)
     return (
         layer_out,
         tokens_grad,
-        tail[E],
-        tail[E + 1],
+        norm_grads[0],
+        norm_grads[1],
         qkv_grad.T,
         mix_grad.T,
-        tail[E + 2],
-        tail[E + 3],
-        tail[:E].T,
+        norm_grads[2],
+        norm_grads[3],
+        router_grad,
         expert_in_grad,
         expert_out_grad,
     )

time: 337 us -> 337 us (level)
    ppermute x21, waiting for transfers between devices: 109 us -> 112 us  [row_swap(): lax.ppermute(x, 'row', swaps('row', k))]
where the time goes in v2:
time: 337 us
  waiting for transfers between devices  161 us (48%)
  Pallas kernels  104 us (31%)
  starting transfers between devices  58.7 us (17%)
  local copies, waits for them, and re-layouts  9.57 us (3%)
    ppermute x21, waiting for transfers between devices, row_swap(): lax.ppermute(x, 'row', swaps('row', k))  112 us
    all_to_all x6, waiting for transfers between devices, exchange(): return lax.all_to_all(pieces, ('row', 'col'), 0, 0, tiled=True)  44.4 us
    ppermute x21, starting transfers between devices, row_swap(): lax.ppermute(x, 'row', swaps('row', k))  22.4 us
    all_to_all x6, starting transfers between devices, exchange(): return lax.all_to_all(pieces, ('row', 'col'), 0, 0, tiled=True)  21.5 us
    pallas_call x1, Pallas kernels, expert_forward(): call(partial(expert_forward_kernel, rows, near), 'expert_forward', (shape...  18.4 us
    pallas_call x1, Pallas kernels, attention_backward(): call(partial(backward_kernel, n, far, parts), 'attention_backward', tuple...  15.3 us
    ppermute x6, starting transfers between devices, far_swap(): lax.ppermute(x, 'col', swaps('col', 2 * k))  14.7 us
    pallas_call x1, Pallas kernels, expert_backward(): call(partial(expert_backward_kernel, rows, near), 'expert_backward', (sha...  12.4 us
  transfers between devices with their start and end apart: 38, of which 22 were waited for; matrix products, arithmetic and copies ran while one was open for 2% of the time, Pallas kernels for 31%

profile of v2, /device:TPU:0, one launch (start us, length us, event | category | flops | bytes accessed | tf_op | source)
XLA Modules:
  0.0 336.6 jit_solution(4909835741338500461)
XLA Ops:
  1.5 5.0 %collective-permute-start.5 = (bf16[256,128]{1,0:T(8,128)(2,1)S(1)}, bf16[256,128]{1,0:T(8,128)(2,1)S(1)}, u32[]{:S(2)}, u32[]{:S(2)}) collective-permute-start(bf16[256,128]{1,0:T(8,128)(2,1)S(1)} %pad_maximum_fusion.1), channel_id=1, source_target_pairs={{0,6},{1,7},{2,4},{3,5},{4,2},{5,3},{6,0},{7,1},{8,14},{9,15},{10,... | collective-permute-start | bytes 196616 | tf_op jit(solution)/shard_map/ppermute | solution.py:108
  7.2 3.8 %pack_weights.1 = bf16[32,128,512]{2,1,0:T(8,128)(2,1)} custom-call(bf16[32,128,256]{2,1,0:T(8,128)(2,1)} %in_ref.1, bf16[32,64,512]{2,1,0:T(8,128)(2,1)} %bitcast.57), custom_call_target="tpu_custom_call" | custom-call | bytes 8388608 | tf_op jit(solution)/shard_map/pack_weights/pallas_call | solution.py:273
  12.3 5.1 %all-to-all-start = ((bf16[32,128,512]{2,1,0:T(8,128)(2,1)}), bf16[32,128,512]{2,1,0:T(8,128)(2,1)}, u32[]{:S(2)}, u32[]{:S(2)}) async-start(bf16[32,128,512]{2,1,0:T(8,128)(2,1)} %pack_weights.1), calls=%async_computation | async-start | bytes 8388608 | tf_op jit(solution)/shard_map/all_to_all | solution.py:37
  17.4 2.7 collective-permute-start.8
  21.0 41.0 %collective-permute-done.8.refs_3_ = bf16[1072,128]{1,0:T(8,128)(2,1)S(1)} collective-permute-done((bf16[1072,128]{1,0:T(8,128)(2,1)S(1)}, bf16[1072,128]{1,0:T(8,128)(2,1)S(1)}, u32[]{:S(2)}, u32[]{:S(2)}) %collective-permute-start.8) | collective-permute-done | bytes 274464 | tf_op jit(solution)/shard_map/ppermute | solution.py:93
  62.8 5.1 %collective-permute-done.6.refs_1_ = bf16[1072,128]{1,0:T(8,128)(2,1)S(1)} collective-permute-done((bf16[1072,128]{1,0:T(8,128)(2,1)S(1)}, bf16[1072,128]{1,0:T(8,128)(2,1)S(1)}, u32[]{:S(2)}, u32[]{:S(2)}) %collective-permute-start.6) | collective-permute-done | bytes 274464 | tf_op jit(solution)/shard_map/ppermute | solution.py:93
  71.0 2.2 collective-permute-start
  73.8 3.3 gather_weights.1
  77.2 2.3 collective-permute-done.1.refs_2_.refs_6_
  79.5 2.2 collective-permute-done.refs_1_.refs_5_
  82.4 8.5 %attention_forward.1 = (bf16[416,128]{1,0:T(8,128)(2,1)}, bf16[416,128]{1,0:T(8,128)(2,1)}, bf16[416,128]{1,0:T(8,128)(2,1)}, bf16[416,128]{1,0:T(8,128)(2,1)}, ...) custom-call(s32[3]{0:T(128)} %pad_add_fusion.where_ref, ...), custom_call_target="tpu_custom_call" | custom-call | flops 1308622848 | bytes 4194304 | tf_op jit(solution)/shard_map/attention_forward/pallas_call | solution.py:516
  92.4 2.0 collective-permute-start.15
  95.4 2.6 collective-permute-done.13.refs_1_
  98.0 1.9 collective-permute-done.15.refs_3_
  100.8 6.3 %dispatch.2 = bf16[3840,128]{1,0:T(8,128)(2,1)} custom-call(s32[3]{0:T(128)S(1)} %copy-done.1, s32[2,1664]{1,0:T(2,128)S(1)} %slots.1.slots_ref, bf16[416,128]{1,0:T(8,128)(2,1)S(1)} %copy-done.9, bf16[416,128]{1,0:T(8,128)(2,1)S(1)} %collective-permute-done.13.refs_1_, bf16[416,128]{1,0:T(8,128)(2,1)S(1)} %collective-permute-done.14.refs_2_, ...), custom_call_target="tpu_custom_call" | custom-call | flops 1635778560 | bytes 1409024 | tf_op jit(solution)/shard_map/dispatch/pallas_call | solution.py:357
  107.1 5.5 %all-to-all-done.w_ref = bf16[32,128,512]{2,1,0:T(8,128)(2,1)} async-done(((bf16[32,128,512]{2,1,0:T(8,128)(2,1)}), bf16[32,128,512]{2,1,0:T(8,128)(2,1)}, u32[]{:S(2)}, u32[]{:S(2)}) %all-to-all-start) | async-done | bytes 4194336 | tf_op jit(solution)/shard_map/all_to_all | solution.py:37
  112.6 4.1 %all-to-all-start.1 = ((bf16[32,120,128]{2,1,0:T(8,128)(2,1)}), bf16[32,120,128]{2,1,0:T(8,128)(2,1)S(1)}, u32[]{:S(2)}, u32[]{:S(2)}) async-start(bf16[32,120,128]{2,1,0:T(8,128)(2,1)} %bitcast.24), calls=%async_computation.1 | async-start | bytes 1966080 | tf_op jit(solution)/shard_map/all_to_all | solution.py:37
  116.6 1.8 collective-permute-start.16
  118.5 1.5 collective-permute-start.17
  120.2 5.7 %dispatch.3 = bf16[3840,128]{1,0:T(8,128)(2,1)} custom-call(s32[1]{0:T(128)} %constant.70.clone.1.where_ref, s32[2,1664]{1,0:T(2,128)S(1)} %slots.1.slots_ref, bf16[1664,128]{1,0:T(8,128)(2,1)S(1)} %bitcast.51), custom_call_target="tpu_custom_call" | custom-call | flops 1635778560 | bytes 1409024 | tf_op jit(solution)/shard_map/dispatch/pallas_call | solution.py:357
  125.9 6.5 %collective-permute-done.16.refs_1_.refs_9_ = bf16[2,416,128]{2,1,0:T(8,128)(2,1)S(1)} collective-permute-done((bf16[2,416,128]{2,1,0:T(8,128)(2,1)}, bf16[2,416,128]{2,1,0:T(8,128)(2,1)S(1)}, u32[]{:S(2)}, u32[]{:S(2)}) %collective-permute-start.16) | collective-permute-done | bytes 213024 | tf_op jit(solution)/shard_map/ppermute | solution.py:93
  133.1 6.6 %collective-permute-done.18.refs_3_.refs_11_ = bf16[2,416,128]{2,1,0:T(8,128)(2,1)S(1)} collective-permute-done((bf16[2,416,128]{2,1,0:T(8,128)(2,1)S(1)}, bf16[2,416,128]{2,1,0:T(8,128)(2,1)S(1)}, u32[]{:S(2)}, u32[]{:S(2)}) %collective-permute-start.18) | collective-permute-done | bytes 213024 | tf_op jit(solution)/shard_map/ppermute | solution.py:93
  140.4 2.4 all-to-all-done.1.got_ref
  142.8 3.4 all-to-all-start.2
  146.2 18.4 %expert_forward.1 = (bf16[32,120,128]{2,1,0:T(8,128)(2,1)}, bf16[960,512]{1,0:T(8,128)(2,1)}, bf16[4,960,512]{2,1,0:T(8,128)(2,1)}, bf16[4,960,512]{2,1,0:T(8,12...) custom-call(s32[1]{0:T(128)} %bitcast.6.e_ref, bf16[32,120,128]{2,1,0:T(8,128)(2,1)} %copy-done.12, ...), custom_call_target="tpu_custom_call" | custom-call | flops 4026531840 | bytes 16777216 | tf_op jit(solution)/shard_map/expert_forward/pallas_call | solution.py:877
  164.6 7.7 %all-to-all-done.2.got_ref = bf16[32,120,128]{2,1,0:T(8,128)(2,1)} async-done(((bf16[32,120,128]{2,1,0:T(8,128)(2,1)}), bf16[32,120,128]{2,1,0:T(8,128)(2,1)}, u32[]{:S(2)}, u32[]{:S(2)}) %all-to-all-start.2) | async-done | bytes 983072 | tf_op jit(solution)/shard_map/all_to_all | solution.py:37
  172.4 2.6 all-to-all-start.3
  175.0 12.4 %expert_backward.1 = (bf16[32,120,128]{2,1,0:T(8,128)(2,1)}, bf16[4,960,512]{2,1,0:T(8,128)(2,1)}, bf16[960,512]{1,0:T(8,128)(2,1)}, f32[32,512]{1,0:T(8,128)}) custom-call(s32[1]{0:T(128)} %bitcast.6.e_ref, bf16[32,120,128]{2,1,0:T(8,128)(2,1)} %all-to-all-done.2.got_ref, bf16[32,128,512]{2,1,0:T(8,128)(2,1)} %all-to-all-done.w_ref, ...), custom_call_target="tpu_custom_call" | custom-call | flops 4026531840 | bytes 16777216 | tf_op jit(solution)/shard_map/expert_backward/pallas_call | solution.py:926
  187.4 13.8 %all-to-all-done.3 = bf16[32,120,128]{2,1,0:T(8,128)(2,1)S(1)} async-done(((bf16[32,120,128]{2,1,0:T(8,128)(2,1)}), bf16[32,120,128]{2,1,0:T(8,128)(2,1)S(1)}, u32[]{:S(2)}, u32[]{:S(2)}) %all-to-all-start.3) | async-done | bytes 983072 | tf_op jit(solution)/shard_map/all_to_all | solution.py:37
  201.2 2.8 all-to-all-start.4
  204.0 11.1 %expert_grads.1 = bf16[32,128,512]{2,1,0:T(8,128)(2,1)} custom-call(bf16[960,512]{1,0:T(8,128)(2,1)} %get-tuple-element.97.x_ref, bf16[4,960,512]{2,1,0:T(8,128)(2,1)} %get-tuple-element.128.pre_ref, bf16[960,512]{1,0:T(8,128)(2,1)} %get-tuple-element.129.grad_res_ref, bf16[4,960,512]{2,1,0:T(8,128)(2,1)} %get-tuple-element.130.act_ref), custom_call_target="tpu_custom_call" | custom-call | flops 4026531840 | bytes 16777216 | tf_op jit(solution)/shard_map/expert_grads/pallas_call | solution.py:968
  215.1 14.9 %all-to-all-done.4 = bf16[32,120,128]{2,1,0:T(8,128)(2,1)S(1)} async-done(((bf16[32,120,128]{2,1,0:T(8,128)(2,1)}), bf16[32,120,128]{2,1,0:T(8,128)(2,1)S(1)}, u32[]{:S(2)}, u32[]{:S(2)}) %all-to-all-start.4) | async-done | bytes 983072 | tf_op jit(solution)/shard_map/all_to_all | solution.py:37
  230.0 3.6 %all-to-all-start.5 = ((bf16[32,128,512]{2,1,0:T(8,128)(2,1)}), bf16[32,128,512]{2,1,0:T(8,128)(2,1)}, u32[]{:S(2)}, u32[]{:S(2)}) async-start(bf16[32,128,512]{2,1,0:T(8,128)(2,1)} %expert_grads.1), calls=%async_computation.5 | async-start | bytes 8388608 | tf_op jit(solution)/shard_map/all_to_all | solution.py:37
  233.6 6.4 %combine.1 = (bf16[416,128]{1,0:T(8,128)(2,1)S(1)}, bf16[416,128]{1,0:T(8,128)(2,1)}, bf16[416,128]{1,0:T(8,128)(2,1)}, bf16[416,128]{1,0:T(8,128)(2,1)}) custom-call(s32[3]{0:T(128)S(1)} %copy-done.1, s32[1664,2]{1,0:T(8,128)S(1)} %bitcast.54, bf16[3840,128]{1,0:T(8,128)(2,1)S(1)} %bitcast.53), custom_call_target="tpu_custom_call" | custom-call | flops 1635778560 | bytes 1409024 | tf_op jit(solution)/shard_map/combine/pallas_call | solution.py:392
  240.0 1.6 collective-permute-start.19
  241.6 1.5 collective-permute-start.20
  243.5 5.8 %finish.1 = bf16[1664,128]{1,0:T(8,128)(2,1)S(1)} custom-call(s32[3]{0:T(128)S(1)} %copy-done.1, s32[1664,2]{1,0:T(8,128)S(1)} %bitcast.55, bf16[3840,128]{1,0:T(8,128)(2,1)S(1)} %bitcast.52, bf16[1664,128]{1,0:T(8,128)(2,1)S(1)} %bitcast.49, bf16[2,416,128]{2,1,0:T(8,128)(2,1)S(1)} %copy-done.8, ...), custom_call_target="tpu_custom_call" | custom-call | flops 1635778560 | bytes 2260992 | tf_op jit(solution)/shard_map/finish/pallas_call | solution.py:422
  250.2 14.4 %collective-permute-done.19.refs_1_ = bf16[416,128]{1,0:T(8,128)(2,1)S(1)} collective-permute-done((bf16[416,128]{1,0:T(8,128)(2,1)}, bf16[416,128]{1,0:T(8,128)(2,1)S(1)}, u32[]{:S(2)}, u32[]{:S(2)}) %collective-permute-start.19) | collective-permute-done | bytes 106528 | tf_op jit(solution)/shard_map/ppermute | solution.py:93
  264.6 7.1 %collective-permute-done.21.refs_3_ = bf16[416,128]{1,0:T(8,128)(2,1)S(1)} collective-permute-done((bf16[416,128]{1,0:T(8,128)(2,1)}, bf16[416,128]{1,0:T(8,128)(2,1)S(1)}, u32[]{:S(2)}, u32[]{:S(2)}) %collective-permute-start.21) | collective-permute-done | bytes 106528 | tf_op jit(solution)/shard_map/ppermute | solution.py:93
  272.3 15.3 %attention_backward.1 = (bf16[416,128]{1,0:T(8,128)(2,1)}, bf16[416,128]{1,0:T(8,128)(2,1)}, bf16[416,128]{1,0:T(8,128)(2,1)}, bf16[416,128]{1,0:T(8,128)(2,1)},...) custom-call(s32[3]{0:T(128)} %pad_add_fusion.where_ref, bf16[416,128]{1,0:T(8,128)(2,1)} %copy-done.10, ...), custom_call_target="tpu_custom_call" | custom-call | flops 3271557120 | bytes 8388608 | tf_op jit(solution)/shard_map/attention_backward/pallas_call | solution.py:669
  287.7 3.1 collective-permute-done.22.got_ref
  293.2 2.8 collective-permute-start.25
  296.6 3.0 collective-permute-done.23
  302.5 8.1 %collective-permute-done.26.refs_1_ = bf16[4,304,128]{2,1,0:T(8,128)(2,1)S(1)} collective-permute-done((bf16[4,304,128]{2,1,0:T(8,128)(2,1)S(1)}, bf16[4,304,128]{2,1,0:T(8,128)(2,1)S(1)}, u32[]{:S(2)}, u32[]{:S(2)}) %collective-permute-start.26) | collective-permute-done | bytes 311328 | tf_op jit(solution)/shard_map/ppermute | solution.py:93
  310.6 9.4 %collective-permute-done.28.refs_3_ = bf16[4,304,128]{2,1,0:T(8,128)(2,1)S(1)} collective-permute-done((bf16[4,304,128]{2,1,0:T(8,128)(2,1)S(1)}, bf16[4,304,128]{2,1,0:T(8,128)(2,1)S(1)}, u32[]{:S(2)}, u32[]{:S(2)}) %collective-permute-start.28) | collective-permute-done | bytes 311328 | tf_op jit(solution)/shard_map/ppermute | solution.py:93
  320.1 6.6 %collective-permute-start.29 = (bf16[304,128]{1,0:T(8,128)(2,1)S(1)}, bf16[304,128]{1,0:T(8,128)(2,1)S(1)}, u32[]{:S(2)}, u32[]{:S(2)}) collective-permute-start(bf16[304,128]{1,0:T(8,128)(2,1)S(1)} %get-tuple-element.134), channel_id=1, source_target_pairs={{0,2},{1,3},{2,0},{3,1},{4,6},{5,7},{6,4},{7,5},{8,10},{9,11},{10,... | collective-permute-start | bytes 233480 | tf_op jit(solution)/shard_map/ppermute | solution.py:108
  327.4 1.8 collective-permute-start.31
  330.2 5.1 %unpack_grads.1 = (f32[32,128,256]{2,1,0:T(8,128)}, f32[32,64,512]{2,1,0:T(8,128)}) custom-call(bf16[32,128,512]{2,1,0:T(8,128)(2,1)} %all-to-all-done.5.got_ref), custom_call_target="tpu_custom_call" | custom-call | bytes 12582912 | tf_op jit(solution)/shard_map/unpack_grads/pallas_call | solution.py:290
  (140 shorter events, 24.9 us)
Async XLA Ops:
  1.5 9.5 %collective-permute-start.5 = (bf16[256,128]{1,0:T(8,128)(2,1)S(1)}, bf16[256,128]{1,0:T(8,128)(2,1)S(1)}, u32[]{:S(2)}, u32[]{:S(2)}) collective-permute-start(bf16[256,128]{1,0:T(8,128)(2,1)S(1)} %pad_maximum_fusion.1), channel_id=1, source_target_pairs={{0,6},{1,7},{2,4},{3,5},{4,2},{5,3},{6,0},{7,1},{8,14},{9,15},{10,... | collective-permute-start | bytes 196616 | tf_op jit(solution)/shard_map/ppermute | solution.py:108
  6.5 5.6 %collective-permute-start.4 = (bf16[256,128]{1,0:T(8,128)(2,1)S(1)}, bf16[256,128]{1,0:T(8,128)(2,1)S(1)}, u32[]{:S(2)}, u32[]{:S(2)}) collective-permute-start(bf16[256,128]{1,0:T(8,128)(2,1)S(1)} %pad_maximum_fusion.1), channel_id=1, source_target_pairs={{0,4},{1,5},{2,6},{3,7},{4,0},{5,1},{6,2},{7,3},{8,12},{9,13},{10,... | collective-permute-start | bytes 196616 | tf_op jit(solution)/shard_map/ppermute | solution.py:108
  6.5 5.6 %collective-permute-start.3 = (bf16[256,128]{1,0:T(8,128)(2,1)S(1)}, bf16[256,128]{1,0:T(8,128)(2,1)S(1)}, u32[]{:S(2)}, u32[]{:S(2)}) collective-permute-start(bf16[256,128]{1,0:T(8,128)(2,1)S(1)} %pad_maximum_fusion.1), channel_id=1, source_target_pairs={{0,2},{1,3},{2,0},{3,1},{4,6},{5,7},{6,4},{7,5},{8,10},{9,11},{10,... | collective-permute-start | bytes 196616 | tf_op jit(solution)/shard_map/ppermute | solution.py:108
  12.3 49.6 %copy-start.13 = (bf16[1576,128]{1,0:T(8,128)(2,1)S(1)}, bf16[1576,128]{1,0:T(8,128)(2,1)}, u32[]{:S(2)}) copy-start(bf16[1576,128]{1,0:T(8,128)(2,1)} %param.13) | copy-start | bytes 1210372
  12.3 56.6 %copy-start.14 = (bf16[1576,128]{1,0:T(8,128)(2,1)S(1)}, bf16[1576,128]{1,0:T(8,128)(2,1)}, u32[]{:S(2)}) copy-start(bf16[1576,128]{1,0:T(8,128)(2,1)} %param.25) | copy-start | bytes 1210372
  12.3 100.2 %all-to-all-start = ((bf16[32,128,512]{2,1,0:T(8,128)(2,1)}), bf16[32,128,512]{2,1,0:T(8,128)(2,1)}, u32[]{:S(2)}, u32[]{:S(2)}) async-start(bf16[32,128,512]{2,1,0:T(8,128)(2,1)} %pack_weights.1), calls=%async_computation | async-start | bytes 8388608 | tf_op jit(solution)/shard_map/all_to_all | solution.py:37
  17.4 44.5 %collective-permute-start.8 = (bf16[1072,128]{1,0:T(8,128)(2,1)S(1)}, bf16[1072,128]{1,0:T(8,128)(2,1)S(1)}, u32[]{:S(2)}, u32[]{:S(2)}) collective-permute-start(bf16[1072,128]{1,0:T(8,128)(2,1)S(1)} %concatenate.11.refs_0_), channel_id=1, source_target_pairs={{0,24},{8,16},{16,8},{24,0},{1,25},{9,17},{17,9},{25,1},{2,26},{10... | collective-permute-start | bytes 823304 | tf_op jit(solution)/shard_map/ppermute | solution.py:93
  20.1 42.7 %collective-permute-start.7 = (bf16[1072,128]{1,0:T(8,128)(2,1)S(1)}, bf16[1072,128]{1,0:T(8,128)(2,1)S(1)}, u32[]{:S(2)}, u32[]{:S(2)}) collective-permute-start(bf16[1072,128]{1,0:T(8,128)(2,1)S(1)} %concatenate.11.refs_0_), channel_id=1, source_target_pairs={{0,16},{8,24},{16,0},{24,8},{1,17},{9,25},{17,1},{25,9},{2,18},{10... | collective-permute-start | bytes 823304 | tf_op jit(solution)/shard_map/ppermute | solution.py:93
  20.6 47.3 %collective-permute-start.6 = (bf16[1072,128]{1,0:T(8,128)(2,1)S(1)}, bf16[1072,128]{1,0:T(8,128)(2,1)S(1)}, u32[]{:S(2)}, u32[]{:S(2)}) collective-permute-start(bf16[1072,128]{1,0:T(8,128)(2,1)S(1)} %concatenate.11.refs_0_), channel_id=1, source_target_pairs={{0,8},{8,0},{16,24},{24,16},{1,9},{9,1},{17,25},{25,17},{2,10},{10... | collective-permute-start | bytes 823304 | tf_op jit(solution)/shard_map/ppermute | solution.py:93
  21.0 48.9 %collective-permute-start.9 = (bf16[1072,128]{1,0:T(8,128)(2,1)S(1)}, bf16[1072,128]{1,0:T(8,128)(2,1)S(1)}, u32[]{:S(2)}, u32[]{:S(2)}) collective-permute-start(bf16[1072,128]{1,0:T(8,128)(2,1)S(1)} %concatenate.11.refs_0_), channel_id=1, source_target_pairs={{0,1},{1,0},{2,3},{3,2},{4,5},{5,4},{6,7},{7,6},{8,9},{9,8},{10,11... | collective-permute-start | bytes 823304 | tf_op jit(solution)/shard_map/ppermute | solution.py:113
  61.9 11.8 %copy-start.15 = (bf16[1072,128]{1,0:T(8,128)(2,1)}, bf16[1072,128]{1,0:T(8,128)(2,1)S(1)}, u32[]{:S(2)}) copy-start(bf16[1072,128]{1,0:T(8,128)(2,1)S(1)} %collective-permute-done.8.refs_3_) | copy-start | bytes 823300
  61.9 9.1 %collective-permute-start.12 = (bf16[1072,128]{1,0:T(8,128)(2,1)S(1)}, bf16[1072,128]{1,0:T(8,128)(2,1)S(1)}, u32[]{:S(2)}, u32[]{:S(2)}) collective-permute-start(bf16[1072,128]{1,0:T(8,128)(2,1)S(1)} %collective-permute-done.8.refs_3_), channel_id=1, source_target_pairs={{0,1},{1,0},{2,3},{3,2},{4,5},{5,4},{6,7},{7,6},{8,9},{9,8},{10,11... | collective-permute-start | bytes 823304 | tf_op jit(solution)/shard_map/ppermute | solution.py:113
  62.8 10.9 %collective-permute-start.11 = (bf16[1072,128]{1,0:T(8,128)(2,1)S(1)}, bf16[1072,128]{1,0:T(8,128)(2,1)}, u32[]{:S(2)}, u32[]{:S(2)}) collective-permute-start(bf16[1072,128]{1,0:T(8,128)(2,1)S(1)} %collective-permute-done.7.refs_2_), channel_id=1, source_target_pairs={{0,1},{1,0},{2,3},{3,2},{4,5},{5,4},{6,7},{7,6},{8,9},{9,8},{10,11... | collective-permute-start | bytes 823304 | tf_op jit(solution)/shard_map/ppermute | solution.py:113
  67.9 5.9 %collective-permute-start.10 = (bf16[1072,128]{1,0:T(8,128)(2,1)S(1)}, bf16[1072,128]{1,0:T(8,128)(2,1)}, u32[]{:S(2)}, u32[]{:S(2)}) collective-permute-start(bf16[1072,128]{1,0:T(8,128)(2,1)S(1)} %collective-permute-done.6.refs_1_), channel_id=1, source_target_pairs={{0,1},{1,0},{2,3},{3,2},{4,5},{5,4},{6,7},{7,6},{8,9},{9,8},{10,11... | collective-permute-start | bytes 823304 | tf_op jit(solution)/shard_map/ppermute | solution.py:113
  68.7 8.5 %collective-permute-start.2 = (bf16[416,128]{1,0:T(8,128)(2,1)}, bf16[416,128]{1,0:T(8,128)(2,1)}, u32[]{:S(2)}, u32[]{:S(2)}) collective-permute-start(bf16[416,128]{1,0:T(8,128)(2,1)} %get-tuple-element.153), channel_id=1, source_target_pairs={{0,24},{8,16},{16,8},{24,0},{1,25},{9,17},{17,9},{25,1},{2,26},{10... | collective-permute-start | bytes 319496 | tf_op jit(solution)/shard_map/ppermute | solution.py:93
  69.1 25.4 %copy-start.22 = (s32[1576,2]{0,1:T(2,128)S(1)}, s32[1576,2]{0,1:T(2,128)}, u32[]{:S(2)}) copy-start(s32[1576,2]{0,1:T(2,128)} %param.23) | copy-start | bytes 37828
  69.1 25.5 %copy-start.23 = (s32[1576,2]{0,1:T(2,128)S(1)}, s32[1576,2]{0,1:T(2,128)}, u32[]{:S(2)}) copy-start(s32[1576,2]{0,1:T(2,128)} %param.24) | copy-start | bytes 37828
  69.9 9.6 %collective-permute-start.1 = (bf16[416,128]{1,0:T(8,128)(2,1)}, bf16[416,128]{1,0:T(8,128)(2,1)S(1)}, u32[]{:S(2)}, u32[]{:S(2)}) collective-permute-start(bf16[416,128]{1,0:T(8,128)(2,1)} %get-tuple-element.154), channel_id=1, source_target_pairs={{0,16},{8,24},{16,0},{24,8},{1,17},{9,25},{17,1},{25,9},{2,18},{10... | collective-permute-start | bytes 319496 | tf_op jit(solution)/shard_map/ppermute | solution.py:93
  71.0 10.7 %collective-permute-start = (bf16[416,128]{1,0:T(8,128)(2,1)S(1)}, bf16[416,128]{1,0:T(8,128)(2,1)S(1)}, u32[]{:S(2)}, u32[]{:S(2)}) collective-permute-start(bf16[416,128]{1,0:T(8,128)(2,1)S(1)} %get-tuple-element.155), channel_id=1, source_target_pairs={{0,8},{8,0},{16,24},{24,16},{1,9},{9,1},{17,25},{25,17},{2,10},{10... | collective-permute-start | bytes 319496 | tf_op jit(solution)/shard_map/ppermute | solution.py:93
  73.8 26.2 %copy-start.1 = (s32[3]{0:T(128)S(1)}, s32[3]{0:T(128)}, u32[]{:S(2)}) copy-start(s32[3]{0:T(128)} %pad_add_fusion.where_ref) | copy-start | bytes 40
  90.9 7.2 %collective-permute-start.13 = (bf16[416,128]{1,0:T(8,128)(2,1)}, bf16[416,128]{1,0:T(8,128)(2,1)S(1)}, u32[]{:S(2)}, u32[]{:S(2)}) collective-permute-start(bf16[416,128]{1,0:T(8,128)(2,1)} %get-tuple-element.84), channel_id=1, source_target_pairs={{0,8},{8,0},{16,24},{24,16},{1,9},{9,1},{17,25},{25,17},{2,10},{10... | collective-permute-start | bytes 319496 | tf_op jit(solution)/shard_map/ppermute | solution.py:93
  91.7 6.4 %collective-permute-start.14 = (bf16[416,128]{1,0:T(8,128)(2,1)}, bf16[416,128]{1,0:T(8,128)(2,1)S(1)}, u32[]{:S(2)}, u32[]{:S(2)}) collective-permute-start(bf16[416,128]{1,0:T(8,128)(2,1)} %get-tuple-element.85), channel_id=1, source_target_pairs={{0,16},{8,24},{16,0},{24,8},{1,17},{9,25},{17,1},{25,9},{2,18},{10... | collective-permute-start | bytes 319496 | tf_op jit(solution)/shard_map/ppermute | solution.py:93
  92.4 7.5 %collective-permute-start.15 = (bf16[416,128]{1,0:T(8,128)(2,1)}, bf16[416,128]{1,0:T(8,128)(2,1)S(1)}, u32[]{:S(2)}, u32[]{:S(2)}) collective-permute-start(bf16[416,128]{1,0:T(8,128)(2,1)} %get-tuple-element.86), channel_id=1, source_target_pairs={{0,24},{8,16},{16,8},{24,0},{1,25},{9,17},{17,9},{25,1},{2,26},{10... | collective-permute-start | bytes 319496 | tf_op jit(solution)/shard_map/ppermute | solution.py:93
  100.8 17.6 %copy-start.30 = (bf16[2,416,128]{2,1,0:T(8,128)(2,1)S(1)}, bf16[2,416,128]{2,1,0:T(8,128)(2,1)}, u32[]{:S(2)}) copy-start(bf16[2,416,128]{2,1,0:T(8,128)(2,1)} %get-tuple-element.93) | copy-start | bytes 638980
  100.8 19.1 %copy-start.29 = (bf16[2,416,128]{2,1,0:T(8,128)(2,1)S(1)}, bf16[2,416,128]{2,1,0:T(8,128)(2,1)}, u32[]{:S(2)}) copy-start(bf16[2,416,128]{2,1,0:T(8,128)(2,1)} %get-tuple-element.94) | copy-start | bytes 638980
  112.6 30.2 %all-to-all-start.1 = ((bf16[32,120,128]{2,1,0:T(8,128)(2,1)}), bf16[32,120,128]{2,1,0:T(8,128)(2,1)S(1)}, u32[]{:S(2)}, u32[]{:S(2)}) async-start(bf16[32,120,128]{2,1,0:T(8,128)(2,1)} %bitcast.24), calls=%async_computation.1 | async-start | bytes 1966080 | tf_op jit(solution)/shard_map/all_to_all | solution.py:37
  116.6 15.8 %collective-permute-start.16 = (bf16[2,416,128]{2,1,0:T(8,128)(2,1)}, bf16[2,416,128]{2,1,0:T(8,128)(2,1)S(1)}, u32[]{:S(2)}, u32[]{:S(2)}) collective-permute-start(bf16[2,416,128]{2,1,0:T(8,128)(2,1)} %get-tuple-element.92), channel_id=1, source_target_pairs={{0,8},{8,0},{16,24},{24,16},{1,9},{9,1},{17,25},{25,17},{2,10},{10... | collective-permute-start | bytes 638984 | tf_op jit(solution)/shard_map/ppermute | solution.py:93
  118.5 13.9 %collective-permute-start.17 = (bf16[2,416,128]{2,1,0:T(8,128)(2,1)S(1)}, bf16[2,416,128]{2,1,0:T(8,128)(2,1)S(1)}, u32[]{:S(2)}, u32[]{:S(2)}) collective-permute-start(bf16[2,416,128]{2,1,0:T(8,128)(2,1)S(1)} %copy-done.30), channel_id=1, source_target_pairs={{0,16},{8,24},{16,0},{24,8},{1,17},{9,25},{17,1},{25,9},{2,18},{10... | collective-permute-start | bytes 638984 | tf_op jit(solution)/shard_map/ppermute | solution.py:93
  119.9 19.8 %collective-permute-start.18 = (bf16[2,416,128]{2,1,0:T(8,128)(2,1)S(1)}, bf16[2,416,128]{2,1,0:T(8,128)(2,1)S(1)}, u32[]{:S(2)}, u32[]{:S(2)}) collective-permute-start(bf16[2,416,128]{2,1,0:T(8,128)(2,1)S(1)} %copy-done.29), channel_id=1, source_target_pairs={{0,24},{8,16},{16,8},{24,0},{1,25},{9,17},{17,9},{25,1},{2,26},{10... | collective-permute-start | bytes 638984 | tf_op jit(solution)/shard_map/ppermute | solution.py:93
  132.4 111.1 %copy-start.3 = (bf16[2,416,128]{2,1,0:T(8,128)(2,1)}, bf16[2,416,128]{2,1,0:T(8,128)(2,1)S(1)}, u32[]{:S(2)}) copy-start(bf16[2,416,128]{2,1,0:T(8,128)(2,1)S(1)} %collective-permute-done.16.refs_1_.refs_9_) | copy-start | bytes 638980
  142.8 29.5 %all-to-all-start.2 = ((bf16[32,120,128]{2,1,0:T(8,128)(2,1)}), bf16[32,120,128]{2,1,0:T(8,128)(2,1)}, u32[]{:S(2)}, u32[]{:S(2)}) async-start(bf16[32,120,128]{2,1,0:T(8,128)(2,1)} %bitcast.27), calls=%async_computation.2 | async-start | bytes 1966080 | tf_op jit(solution)/shard_map/all_to_all | solution.py:37
  172.4 28.8 %all-to-all-start.3 = ((bf16[32,120,128]{2,1,0:T(8,128)(2,1)}), bf16[32,120,128]{2,1,0:T(8,128)(2,1)S(1)}, u32[]{:S(2)}, u32[]{:S(2)}) async-start(bf16[32,120,128]{2,1,0:T(8,128)(2,1)} %get-tuple-element.96), calls=%async_computation.3 | async-start | bytes 1966080 | tf_op jit(solution)/shard_map/all_to_all | solution.py:37
  201.2 28.8 %all-to-all-start.4 = ((bf16[32,120,128]{2,1,0:T(8,128)(2,1)}), bf16[32,120,128]{2,1,0:T(8,128)(2,1)S(1)}, u32[]{:S(2)}, u32[]{:S(2)}) async-start(bf16[32,120,128]{2,1,0:T(8,128)(2,1)} %get-tuple-element.102), calls=%async_computation.4 | async-start | bytes 1966080 | tf_op jit(solution)/shard_map/all_to_all | solution.py:37
  230.0 100.1 %all-to-all-start.5 = ((bf16[32,128,512]{2,1,0:T(8,128)(2,1)}), bf16[32,128,512]{2,1,0:T(8,128)(2,1)}, u32[]{:S(2)}, u32[]{:S(2)}) async-start(bf16[32,128,512]{2,1,0:T(8,128)(2,1)} %expert_grads.1), calls=%async_computation.5 | async-start | bytes 8388608 | tf_op jit(solution)/shard_map/all_to_all | solution.py:37
  240.0 24.6 %collective-permute-start.19 = (bf16[416,128]{1,0:T(8,128)(2,1)}, bf16[416,128]{1,0:T(8,128)(2,1)S(1)}, u32[]{:S(2)}, u32[]{:S(2)}) collective-permute-start(bf16[416,128]{1,0:T(8,128)(2,1)} %get-tuple-element.105), channel_id=1, source_target_pairs={{0,8},{8,0},{16,24},{24,16},{1,9},{9,1},{17,25},{25,17},{2,10},{10... | collective-permute-start | bytes 319496 | tf_op jit(solution)/shard_map/ppermute | solution.py:93
  241.6 23.0 %collective-permute-start.20 = (bf16[416,128]{1,0:T(8,128)(2,1)}, bf16[416,128]{1,0:T(8,128)(2,1)S(1)}, u32[]{:S(2)}, u32[]{:S(2)}) collective-permute-start(bf16[416,128]{1,0:T(8,128)(2,1)} %get-tuple-element.106), channel_id=1, source_target_pairs={{0,16},{8,24},{16,0},{24,8},{1,17},{9,25},{17,1},{25,9},{2,18},{10... | collective-permute-start | bytes 319496 | tf_op jit(solution)/shard_map/ppermute | solution.py:93
  243.1 28.6 %collective-permute-start.21 = (bf16[416,128]{1,0:T(8,128)(2,1)}, bf16[416,128]{1,0:T(8,128)(2,1)S(1)}, u32[]{:S(2)}, u32[]{:S(2)}) collective-permute-start(bf16[416,128]{1,0:T(8,128)(2,1)} %get-tuple-element.107), channel_id=1, source_target_pairs={{0,24},{8,16},{16,8},{24,0},{1,25},{9,17},{17,9},{25,1},{2,26},{10... | collective-permute-start | bytes 319496 | tf_op jit(solution)/shard_map/ppermute | solution.py:93
  287.6 3.2 collective-permute-start.22
  292.4 7.3 %collective-permute-start.23 = (bf16[416,128]{1,0:T(8,128)(2,1)}, bf16[416,128]{1,0:T(8,128)(2,1)S(1)}, u32[]{:S(2)}, u32[]{:S(2)}) collective-permute-start(bf16[416,128]{1,0:T(8,128)(2,1)} %get-tuple-element.120), channel_id=1, source_target_pairs={{0,24},{8,16},{16,8},{24,0},{1,25},{9,17},{17,9},{25,1},{2,26},{10... | collective-permute-start | bytes 319496 | tf_op jit(solution)/shard_map/ppermute | solution.py:93
  292.5 9.0 %collective-permute-start.24 = (bf16[416,128]{1,0:T(8,128)(2,1)}, bf16[416,128]{1,0:T(8,128)(2,1)S(1)}, u32[]{:S(2)}, u32[]{:S(2)}) collective-permute-start(bf16[416,128]{1,0:T(8,128)(2,1)} %get-tuple-element.122), channel_id=1, source_target_pairs={{0,16},{8,24},{16,0},{24,8},{1,17},{9,25},{17,1},{25,9},{2,18},{10... | collective-permute-start | bytes 319496 | tf_op jit(solution)/shard_map/ppermute | solution.py:93
  293.2 8.3 %collective-permute-start.25 = (bf16[416,128]{1,0:T(8,128)(2,1)}, bf16[416,128]{1,0:T(8,128)(2,1)S(1)}, u32[]{:S(2)}, u32[]{:S(2)}) collective-permute-start(bf16[416,128]{1,0:T(8,128)(2,1)} %get-tuple-element.124), channel_id=1, source_target_pairs={{0,8},{8,0},{16,24},{24,16},{1,9},{9,1},{17,25},{25,17},{2,10},{10... | collective-permute-start | bytes 319496 | tf_op jit(solution)/shard_map/ppermute | solution.py:93
  295.9 14.6 %collective-permute-start.26 = (bf16[4,304,128]{2,1,0:T(8,128)(2,1)S(1)}, bf16[4,304,128]{2,1,0:T(8,128)(2,1)S(1)}, u32[]{:S(2)}, u32[]{:S(2)}) collective-permute-start(bf16[4,304,128]{2,1,0:T(8,128)(2,1)S(1)} %get-tuple-element.117), channel_id=1, source_target_pairs={{0,8},{8,0},{16,24},{24,16},{1,9},{9,1},{17,25},{25,17},{2,10},{10... | collective-permute-start | bytes 933896 | tf_op jit(solution)/shard_map/ppermute | solution.py:93
  296.0 14.6 %collective-permute-start.27 = (bf16[4,304,128]{2,1,0:T(8,128)(2,1)S(1)}, bf16[4,304,128]{2,1,0:T(8,128)(2,1)S(1)}, u32[]{:S(2)}, u32[]{:S(2)}) collective-permute-start(bf16[4,304,128]{2,1,0:T(8,128)(2,1)S(1)} %get-tuple-element.118), channel_id=1, source_target_pairs={{0,16},{8,24},{16,0},{24,8},{1,17},{9,25},{17,1},{25,9},{2,18},{10... | collective-permute-start | bytes 933896 | tf_op jit(solution)/shard_map/ppermute | solution.py:93
  299.6 20.3 %collective-permute-start.28 = (bf16[4,304,128]{2,1,0:T(8,128)(2,1)S(1)}, bf16[4,304,128]{2,1,0:T(8,128)(2,1)S(1)}, u32[]{:S(2)}, u32[]{:S(2)}) collective-permute-start(bf16[4,304,128]{2,1,0:T(8,128)(2,1)S(1)} %get-tuple-element.119), channel_id=1, source_target_pairs={{0,24},{8,16},{16,8},{24,0},{1,25},{9,17},{17,9},{25,1},{2,26},{10... | collective-permute-start | bytes 933896 | tf_op jit(solution)/shard_map/ppermute | solution.py:93
  302.4 32.8 %copy-start.2 = (s32[3]{0:T(128)S(1)}, s32[3]{0:T(128)}, u32[]{:S(2)}) copy-start(s32[3]{0:T(128)} %pad_add_fusion.where_ref) | copy-start | bytes 40
  320.1 15.1 %collective-permute-start.29 = (bf16[304,128]{1,0:T(8,128)(2,1)S(1)}, bf16[304,128]{1,0:T(8,128)(2,1)S(1)}, u32[]{:S(2)}, u32[]{:S(2)}) collective-permute-start(bf16[304,128]{1,0:T(8,128)(2,1)S(1)} %get-tuple-element.134), channel_id=1, source_target_pairs={{0,2},{1,3},{2,0},{3,1},{4,6},{5,7},{6,4},{7,5},{8,10},{9,11},{10,... | collective-permute-start | bytes 233480 | tf_op jit(solution)/shard_map/ppermute | solution.py:108
  326.7 8.6 %collective-permute-start.30 = (bf16[304,128]{1,0:T(8,128)(2,1)S(1)}, bf16[304,128]{1,0:T(8,128)(2,1)S(1)}, u32[]{:S(2)}, u32[]{:S(2)}) collective-permute-start(bf16[304,128]{1,0:T(8,128)(2,1)S(1)} %get-tuple-element.135), channel_id=1, source_target_pairs={{0,4},{1,5},{2,6},{3,7},{4,0},{5,1},{6,2},{7,3},{8,12},{9,13},{10,... | collective-permute-start | bytes 233480 | tf_op jit(solution)/shard_map/ppermute | solution.py:108
  327.4 7.9 %collective-permute-start.31 = (bf16[304,128]{1,0:T(8,128)(2,1)S(1)}, bf16[304,128]{1,0:T(8,128)(2,1)S(1)}, u32[]{:S(2)}, u32[]{:S(2)}) collective-permute-start(bf16[304,128]{1,0:T(8,128)(2,1)S(1)} %get-tuple-element.136), channel_id=1, source_target_pairs={{0,6},{1,7},{2,4},{3,5},{4,2},{5,3},{6,0},{7,1},{8,14},{9,15},{10,... | collective-permute-start | bytes 233480 | tf_op jit(solution)/shard_map/ppermute | solution.py:108
  (26 other events, 126.2 us)
